TPU v7x, 128 devices: a whole 4x4x4 slice. The times are simulated.
128 devices in a mesh: prow: 8 (over x, core), pcol: 16 (over z, y).
Axes of the slice: x: 4, y: 4, z: 4, core: 2. Of those that a mesh axis runs over, the one named last changes fastest.
Arguments:
- matrix: float32 [8, 16, 768, 384], P('prow', 'pcol'), may hold values from -6 to 6
- pivots: int32 [3, 384], replicated, may hold values from 0 to 6143, as said below
- lower_inv: float32 [3, 384, 384], replicated, may hold values from -0.3125 to 0.3125
- upper_inv: float32 [3, 384, 384], replicated, may hold values from -0.015625 to 0.015625
Outputs:
- factored: float32 [8, 16, 768, 384], P('prow', 'pcol')
Inputs may be any that keep to these rules, and one draw needn't show every extreme that they name: Within one step s the indices pivots[s, i] are distinct, and each equals s * 384 + i or lies between (s + 1) * 384 and 6143.
All inputs are finite; a program needn't handle non-finite values.
Results may differ from a plain program's by a relative error of at most 0.0002.
Values sent between devices are 32-bit elements; how exact they have to be, the bound alone decides.
No kernel may reach another device: no remote copies, remote signals or barrier semaphores. Data moves between devices by JAX's collectives and lax.ppermute only.
A program may use at most 64 MiB of HBM per device.

v0:
```python
import jax
import jax.numpy as jnp
from jax import lax
from jax.experimental import pallas as pl
from jax.experimental.pallas import tpu as pltpu
from jax.sharding import PartitionSpec as P

W = 384
STEPS = 3
NX, NZ, NY = 4, 4, 4
PROWS, PCOLS = 8, 16
TOP = STEPS * W
SUB = W // PROWS
COLS = W // PCOLS
ROWS = 2 * W
F32 = jnp.float32
BF16 = jnp.bfloat16


def x_shift(v, k):
    return lax.ppermute(v, "prow", [(p, (p + 2 * k) % PROWS) for p in range(PROWS)])


def x_shift_top(v, k):
    return lax.ppermute(v, "prow", [(p, (p + 2 * k) % PROWS) for p in range(STEPS)])


def sibling(v):
    return lax.ppermute(v, "prow", [(p, p ^ 1) for p in range(PROWS)])


def to_odd(v):
    return lax.ppermute(v, "prow", [(p, p + 1) for p in range(0, PROWS, 2)])


def y_shift(v, k):
    return lax.ppermute(
        v, "pcol", [(z * NY + y, z * NY + (y + k) % NY) for z in range(NZ) for y in range(NY)]
    )


def from_z0(v, k):
    return lax.ppermute(v, "pcol", [(y, k * NY + y) for y in range(STEPS)])


def after(v, *others):
    return lax.optimization_barrier((v, *others))[0]


def placed(parts, places, axis):
    shape = parts[0].shape
    whole = jnp.zeros(shape[:axis] + (len(parts),) + shape[axis:], parts[0].dtype)
    for part, place in zip(parts, places):
        whole = lax.dynamic_update_slice_in_dim(whole, jnp.expand_dims(part, axis), place, axis=axis)
    return whole


def tops_by_x(block, got, x, core):
    first = jnp.where(x == 0, block, 0) + jnp.where(x == 1, got[0], 0)
    first = first + jnp.where(x == 2, got[1], 0) + jnp.where(x == 3, got[2], 0)
    even = core == 0
    second = jnp.where((x == 1) & even, block, 0) + jnp.where((x == 2) & even, got[0], 0)
    second = second + jnp.where((x == 3) & even, got[1], 0) + jnp.where((x == 0) & even, got[2], 0)
    return first, second


def halves(v):
    high = v.astype(BF16)
    return high, (v - high.astype(F32)).astype(BF16)


def thirds(v):
    high = v.astype(BF16).astype(F32)
    rest = v - high
    middle = rest.astype(BF16).astype(F32)
    return high, middle, rest - middle


def dot(u, v):
    return jnp.dot(u, v, preferred_element_type=F32)


def mm3(a, b):
    return dot(a[0], b[0]) + (dot(a[0], b[1]) + dot(a[1], b[0]))


def lhs3(v):
    high, low = v if isinstance(v, tuple) else halves(v)
    return jnp.concatenate([high, high, low], axis=1)


def rhs3(v):
    high, low = v if isinstance(v, tuple) else halves(v)
    return jnp.concatenate([high, low, high], axis=0)


def origin(v, pivots_ref, axis):
    for section in reversed(range(STEPS)):
        if axis == 1:
            listed = pivots_ref[section : section + 1, :].astype(F32)
        else:
            listed = pivots_ref[:, section : section + 1].astype(F32)
        shape = listed.shape
        here = (lax.broadcasted_iota(jnp.int32, shape, axis) + section * W).astype(F32)
        moves = jnp.where(v == listed, here - v, 0.0) + jnp.where(v == here, listed - v, 0.0)
        v = v + jnp.sum(moves, axis=axis, keepdims=True)
    return v


def third_of(n):
    return (n * 43) >> 7


def picking_kernel(facts_ref, pivots_ref, tile_ref, near_ref, far_ref, chosen_ref):
    p, x, core = facts_ref[0], facts_ref[1], facts_ref[2]
    size = STEPS * SUB
    row = lax.broadcasted_iota(jnp.int32, (size, 1), 0)
    late = (row >= SUB).astype(jnp.int32) + (row >= 2 * SUB).astype(jnp.int32)
    base = row + late * (W - SUB)
    for side in range(2):
        for k in range(NX):
            piece = ((x + k) % NX) * 2 + (core ^ side)
            source = origin((base + piece * SUB).astype(F32), pivots_ref, 1).astype(jnp.int32)
            block = third_of(source >> 7)
            local = source - block * W + (block >> 3) * W
            local = jnp.where((block & 7) == p, local, -1)
            spots = lax.broadcasted_iota(jnp.int32, (size, ROWS), 1)
            at = (side * NX + k) * size
            chosen_ref[at : at + size, :] = (local == spots).astype(F32).astype(BF16)
    high, middle, low = (part.astype(BF16) for part in thirds(tile_ref[...]))
    half = NX * size
    for out_ref, at in ((far_ref, half), (near_ref, 0)):
        chosen = chosen_ref[at : at + half, :]
        out_ref[...] = dot(chosen, low) + dot(chosen, middle) + dot(chosen, high)


def table_place(came, ids_global, core):
    swapped = jnp.where(came < W, came + W, came - W)
    place = jnp.where((core == 1) & (came < 2 * W), swapped, came)
    return jnp.where((ids_global >= TOP) & (came < TOP), place, -1)


def globals_of(ids, p):
    return ids + p * W + jnp.where(ids >= W, (PROWS - 1) * W, 0)


def strips_kernel(facts_ref, pivots_ref, strips_ref, a_ref, other_ref, b_ref, far_ref, out_ref):
    p, core = facts_ref[0], facts_ref[2]
    ids = globals_of(lax.broadcasted_iota(jnp.int32, (1, ROWS), 1), p)
    came = origin(ids.astype(F32), pivots_ref, 0).astype(jnp.int32)
    place = table_place(came, ids, core)
    spots = lax.broadcasted_iota(jnp.int32, (TOP, ROWS), 0)
    chosen = (spots == place).astype(F32).astype(BF16)
    last = jnp.where(core == 0, b_ref[...], far_ref[...])
    parts = thirds(jnp.concatenate([a_ref[...], other_ref[...], last], axis=1))
    size = parts[0].shape[0]
    stacked = jnp.concatenate(parts + (jnp.zeros((8, TOP), F32),), axis=0).astype(BF16)
    found = dot(stacked, chosen)
    found = found[2 * size : 3 * size] + found[size : 2 * size] + found[:size]
    out_ref[...] = jnp.where(place >= 0, found, strips_ref[...])


def rows_kernel(facts_ref, pivots_ref, tile_ref, tops_ref, out_ref, tops, sem):
    copy = pltpu.make_async_copy(tops_ref.at[:STEPS], tops, sem)
    copy.start()
    p = facts_ref[0]
    ids = globals_of(lax.broadcasted_iota(jnp.int32, (ROWS, 1), 0), p)
    came = origin(ids.astype(F32), pivots_ref, 1).astype(jnp.int32)
    place = table_place(came, ids, 0)
    spots = lax.broadcasted_iota(jnp.int32, (ROWS, TOP), 1)
    chosen = (spots == place).astype(F32).astype(BF16)
    copy.wait()
    high, middle, low = (part.astype(BF16) for part in thirds(tops[...].reshape(TOP, W)))
    found = dot(chosen, low) + dot(chosen, middle) + dot(chosen, high)
    out_ref[...] = jnp.where(place >= 0, found, tile_ref[...])


def triangles_kernel(lower_ref, upper_ref, low_ref, low2_ref, up_ref, up2_ref, tri, sems):
    row = lax.broadcasted_iota(jnp.int32, (W, W), 0)
    col = lax.broadcasted_iota(jnp.int32, (W, W), 1)
    for s in range(STEPS):
        tri[0, s], tri[1, s] = halves(jnp.where(row > col, lower_ref[s], (row == col).astype(F32)))
        tri[2, s], tri[3, s] = halves(jnp.where(row <= col, upper_ref[s], 0.0))
    copies = [
        pltpu.make_async_copy(tri.at[i], ref, sems.at[i])
        for i, ref in enumerate((low_ref, low2_ref, up_ref, up2_ref))
    ]
    for copy in copies:
        copy.start()
    for copy in copies:
        copy.wait()


def factor_kernel(facts_ref, *refs):
    pieces, nears = refs[:PROWS], refs[PROWS : 2 * PROWS]
    triangles = refs[2 * PROWS : 2 * PROWS + 4]
    basis_ref, head_ref, corner, own, tri, sems = refs[2 * PROWS + 4 :]
    copies = []
    for i in range(4):
        copies.append(pltpu.make_async_copy(triangles[i], tri.at[i], sems.at[2 * PROWS + i]))
    for i in range(PROWS):
        spot = pl.ds(pl.multiple_of(facts_ref[3 + i] * SUB, 16), SUB)
        copies.append(pltpu.make_async_copy(pieces[i], corner.at[:, :, spot, :], sems.at[2 * i]))
        copies.append(pltpu.make_async_copy(nears[i], own.at[:, spot, :], sems.at[2 * i + 1]))
    for copy in copies:
        copy.start()
    p, q = facts_ref[0], facts_ref[11]
    row = lax.broadcasted_iota(jnp.int32, (W, W), 0)
    col = lax.broadcasted_iota(jnp.int32, (W, W), 1)
    eye = (row == col).astype(F32)
    for copy in copies:
        copy.wait()
    low = [(tri[0, s], tri[1, s]) for s in range(STEPS)]
    up = [(tri[2, s], tri[3, s]) for s in range(STEPS)]
    z0 = own[0]
    wide = jnp.concatenate([corner[1, 1], corner[2, 0], z0], axis=1)
    wide = dot(lhs3(low[0]), rhs3(wide))
    wide3 = rhs3(wide)
    u01, u02, u0 = wide[:, :W], wide[:, W : 2 * W], wide[:, 2 * W :]
    tall = jnp.concatenate([corner[0, 0], corner[0, 1]], axis=0)
    tall = dot(lhs3(tall), rhs3(up[0]))
    l10, l20 = tall[:W], tall[W:]
    both = jnp.concatenate([corner[2, 1], own[1]], axis=1) - dot(lhs3(l10), wide3[:, W:])
    x1 = both[:, W:]
    both = dot(lhs3(low[1]), rhs3(both))
    u12, u1 = both[:, :W], both[:, W:]
    l20_3 = lhs3(l20)
    l21 = dot(lhs3(corner[1, 0] - dot(l20_3, wide3[:, :W])), rhs3(up[1]))
    x2 = own[2] - dot(l20_3, wide3[:, 2 * W :]) - dot(lhs3(l21), rhs3(u1))
    u2 = dot(lhs3(low[2]), rhs3(x2))

    @pl.when(p == 0)
    def _():
        head_ref[...] = jnp.where(q == 0, z0, u0)

    @pl.when(p == 1)
    def _():
        head_ref[...] = jnp.where(q == 0, l10, jnp.where(q == 1, x1, u1))

    @pl.when(p >= 2)
    def _():
        head_ref[...] = jnp.where(q == 0, l20, jnp.where(q == 1, l21, jnp.where(q == 2, x2, u2)))

    def basis(t, value):
        return jnp.where(q >= STEPS, value, jnp.where(q == t, -eye, 0.0))

    def keep(t, value):
        for j in range(PCOLS):
            at = (j * STEPS + t) * COLS
            basis_ref[at : at + COLS, :] = value[j * COLS : (j + 1) * COLS, :]

    g2 = dot(lhs3(up[2]), rhs3(basis(2, u2)))
    keep(2, g2)
    g2_3 = rhs3(g2)
    g1 = dot(lhs3(up[1]), rhs3(basis(1, u1) - dot(lhs3(u12), g2_3)))
    keep(1, g1)
    left = jnp.concatenate([lhs3(u01), lhs3(u02)], axis=1)
    right = jnp.concatenate([rhs3(g1), g2_3], axis=0)
    g0 = dot(lhs3(up[0]), rhs3(basis(0, u0) - dot(left, right)))
    keep(0, g0)


def final_kernel(facts_ref, panel_ref, basis_ref, here_ref, head_ref, out_ref, panel, sems):
    p, q = facts_ref[0], facts_ref[11]
    copies = [
        pltpu.make_async_copy(panel_ref.at[:, i * W : (i + 1) * W], panel.at[i], sems.at[i])
        for i in range(2)
    ]
    for copy in copies:
        copy.start()
    g = halves(basis_ref[...])

    def rows(i):
        span = slice(i * W, (i + 1) * W)
        a = halves(panel[i].T)
        out_ref[span, :] = jnp.where(q >= STEPS, here_ref[span, :], 0.0) - mm3(a, g)

    copies[0].wait()

    @pl.when(p < STEPS)
    def _():
        out_ref[:W, :] = head_ref[...]

    @pl.when(p >= STEPS)
    def _():
        rows(0)

    copies[1].wait()
    rows(1)


SMEM = pl.BlockSpec(memory_space=pltpu.SMEM)
WHOLE = pl.BlockSpec()
HBM = pl.BlockSpec(memory_space=pltpu.HBM)


def cost(flops, moved):
    return pl.CostEstimate(flops=flops, bytes_accessed=moved, transcendentals=0)


def shape(*sizes):
    return jax.ShapeDtypeStruct(sizes, F32)


def params(mib):
    return pltpu.CompilerParams(vmem_limit_bytes=mib << 20)


def on_device(matrix, pivots, lower_inv, upper_inv):
    p = lax.axis_index("prow")
    q = lax.axis_index("pcol")
    x, core = p // 2, p % 2
    z, y = q // NY, q % NY
    tile = matrix[0, 0]
    held = [(x - k) % NX * 2 + (core ^ side) for side in (0, 1) for k in range(NX)]
    facts = jnp.stack([p, x, core] + held + [q]).astype(jnp.int32)

    flat = tile.T
    got = [from_z0(flat[k * (W // NZ) : (k + 1) * (W // NZ)], k) for k in (1, 2, 3)]

    own_tops = lax.all_gather(tile[:W], "prow")

    kept, sent = pl.pallas_call(
        picking_kernel,
        out_shape=(shape(ROWS // 4 * 3, W),) * 2,
        in_specs=[SMEM, WHOLE, WHOLE],
        scratch_shapes=[pltpu.VMEM((TOP, ROWS), BF16)],
        compiler_params=params(14),
        cost_estimate=cost(2 * TOP * ROWS * TOP, 3 << 20),
    )(facts, pivots, tile)

    *got, kept, sent = lax.optimization_barrier((*got, kept, sent))
    crossed = sibling(sent)
    part = jnp.where(z == 0, flat[: W // NZ], 0.0)
    for v in got:
        part = part + v
    part = part.reshape(NY, COLS, ROWS)
    cut = [lax.dynamic_index_in_dim(part, (y + k) % NY, keepdims=False) for k in range(NY)]
    got = [y_shift(cut[k], k) for k in (1, 2, 3)]

    triangles = pl.pallas_call(
        triangles_kernel,
        out_shape=(jax.ShapeDtypeStruct((STEPS, W, W), BF16),) * 4,
        in_specs=[WHOLE] * 2,
        out_specs=(HBM,) * 4,
        scratch_shapes=[pltpu.VMEM((4, STEPS, W, W), BF16), pltpu.SemaphoreType.DMA((4,))],
        compiler_params=params(16),
        cost_estimate=cost(1 << 23, 7 << 20),
    )(lower_inv, upper_inv)

    *got, crossed, t1, t2, t3, t4 = lax.optimization_barrier((*got, crossed, *triangles))
    triangles = (t1, t2, t3, t4)
    summed = (kept + crossed).reshape(NX, STEPS * SUB, W)
    strips = placed(cut[:1] + got, [(y - k) % NY for k in range(NY)], 0)[:STEPS]
    strips = strips.reshape(STEPS * COLS, ROWS)
    strip_tops = strips[:, :W]
    tops_got = [x_shift_top(strip_tops, k) for k in (1, 2, 3)]

    around = [x_shift(summed[k], k) for k in (1, 2, 3)]

    *tops_got, summed = lax.optimization_barrier((*tops_got, summed))
    a, b = tops_by_x(strip_tops, tops_got, x, core)
    a_other, b_far = sibling(a), to_odd(b)

    *around, a_other, b_far = lax.optimization_barrier((*around, a_other, b_far))
    strips = pl.pallas_call(
        strips_kernel,
        out_shape=shape(STEPS * COLS, ROWS),
        in_specs=[SMEM] + [WHOLE] * 6,
        compiler_params=params(14),
        cost_estimate=cost(2 * 216 * TOP * ROWS, 1 << 20),
    )(facts, pivots.T, strips, a, a_other, b, b_far)
    panel = lax.all_gather(strips, "pcol").reshape(TOP, ROWS)
    chunk = summed[0]
    for v in around:
        chunk = chunk + v
    parts = chunk.reshape(STEPS, SUB, W)
    twice = jnp.concatenate([parts, parts])
    off = lax.dynamic_slice_in_dim(twice, (y + 1) % STEPS, 2, axis=0)
    got = [from_z0(off, k) for k in (1, 2, 3)]
    near = [parts] + [x_shift(parts, k) for k in (1, 2, 3)]

    got_near = lax.optimization_barrier((*got, strips, *near))
    got, strips, near = got_near[:3], got_near[3], list(got_near[4:])
    near = near + [sibling(v) for v in near]
    spread = jnp.where(z == 0, off, 0.0)
    for v in got:
        spread = spread + v
    line = [spread] + [y_shift(spread, k) for k in (1, 2, 3)]
    line = placed(line, [(y - k) % NY for k in range(NY)], 0)[:STEPS]
    ring = [line] + [x_shift(line, k) for k in (1, 2, 3)]

    here = pl.pallas_call(
        rows_kernel,
        out_shape=shape(ROWS, W),
        in_specs=[SMEM, WHOLE, WHOLE, HBM],
        scratch_shapes=[pltpu.VMEM((STEPS, W, W), F32), pltpu.SemaphoreType.DMA],
        compiler_params=params(60),
        cost_estimate=cost(2 * ROWS * TOP * TOP, 5 << 20),
    )(facts, pivots, tile, own_tops)

    *ring, here = lax.optimization_barrier((*ring, here))
    ring = ring + [sibling(v) for v in ring]

    basis, head = pl.pallas_call(
        factor_kernel,
        out_shape=(shape(TOP, W), shape(W, W)),
        in_specs=[SMEM] + [HBM] * (2 * PROWS + 4),
        scratch_shapes=[
            pltpu.VMEM((STEPS, 2, W, W), F32),
            pltpu.VMEM((STEPS, W, W), F32),
            pltpu.VMEM((4, STEPS, W, W), BF16),
            pltpu.SemaphoreType.DMA((2 * PROWS + 4,)),
        ],
        compiler_params=params(60),
        cost_estimate=cost(40 * 3 * W**3, 11 << 20),
    )(facts, *ring, *near, *triangles)

    result = pl.pallas_call(
        final_kernel,
        out_shape=shape(ROWS, W),
        in_specs=[SMEM, HBM] + [WHOLE] * 3,
        scratch_shapes=[pltpu.VMEM((2, TOP, W), F32), pltpu.SemaphoreType.DMA((2,))],
        compiler_params=params(60),
        cost_estimate=cost(6 * ROWS * TOP * W, 8 << 20),
    )(facts, panel, basis, here, head)
    return result[None, None]


def solution(mesh):
    return jax.shard_map(
        on_device,
        mesh=mesh,
        in_specs=(P("prow", "pcol", None, None), P(), P(), P()),
        out_specs=P("prow", "pcol", None, None),
        check_vma=False,
    )
```

profile of v0, /device:TPU:11, one launch (start us, length us, event | category | flops | bytes accessed | tf_op | source)
XLA Modules:
  0.0 146.6 jit_solution(16407494541714382961)
XLA Ops:
  6.5 2.0 %slice.51 = f32[1,1,384,384]{3,2,1,0:T(8,128)} slice(f32[1,1,768,384]{3,2,1,0:T(8,128)} %param.4), slice={[0:1], [0:1], [0:384], [0:384]} | slice | bytes 1179648 | tf_op jit(solution)/shard_map/slice | solution.py:321
  9.0 3.6 %collective-permute-start = (f32[96,768]{0,1:T(8,128)S(1)}, f32[96,768]{0,1:T(8,128)S(1)}, u32[]{:S(2)}, u32[]{:S(2)}) collective-permute-start(f32[96,768]{0,1:T(8,128)S(1)} %get-tuple-element.93), channel_id=1, source_target_pairs={{0,4},{1,5},{2,6},{16,20},{17,21},{18,22},{32,36},{33,37},{34,38},... | collective-permute-start | bytes 884744 | tf_op jit(solution)/shard_map/ppermute | solution.py:43
  12.6 2.6 %collective-permute-start.1 = (f32[96,768]{0,1:T(8,128)S(1)}, f32[96,768]{0,1:T(8,128)S(1)}, u32[]{:S(2)}, u32[]{:S(2)}) collective-permute-start(f32[96,768]{0,1:T(8,128)S(1)} %get-tuple-element.92), channel_id=1, source_target_pairs={{0,8},{1,9},{2,10},{16,24},{17,25},{18,26},{32,40},{33,41},{34,42}... | collective-permute-start | bytes 884744 | tf_op jit(solution)/shard_map/ppermute | solution.py:43
  16.8 4.5 %shard_map.46 = (f32[576,384]{1,0:T(8,128)S(1)}, f32[576,384]{1,0:T(8,128)}) custom-call(s32[12]{0:T(128)S(1)} %stack.51.facts_ref, s32[3,384]{1,0:T(4,128)S(1)} %copy-done.5, f32[768,384]{1,0:T(8,128)S(1)} %bitcast.50), custom_call_target="tpu_custom_call" | custom-call | flops 2038431744 | bytes 3145728 | tf_op jit(solution)/shard_map/pallas_call | solution.py:323
  22.2 6.5 %collective-permute-done.1 = f32[96,768]{0,1:T(8,128)S(1)} collective-permute-done((f32[96,768]{0,1:T(8,128)S(1)}, f32[96,768]{0,1:T(8,128)S(1)}, u32[]{:S(2)}, u32[]{:S(2)}) %collective-permute-start.1) | collective-permute-done | bytes 294944 | tf_op jit(solution)/shard_map/ppermute | solution.py:43
  28.8 1.5 %collective-permute-start.6 = (f32[576,384]{1,0:T(8,128)}, f32[576,384]{1,0:T(8,128)}, u32[]{:S(2)}, u32[]{:S(2)}) collective-permute-start(f32[576,384]{1,0:T(8,128)} %get-tuple-element.52), channel_id=1, source_target_pairs={{0,16},{16,0},{32,48},{48,32},{64,80},{80,64},{96,112},{112,96},{1... | collective-permute-start | bytes 2654216 | tf_op jit(solution)/shard_map/ppermute | solution.py:29
  43.8 4.8 %collective-permute-start.11 = (f32[144,384]{1,0:T(8,128)S(1)}, f32[144,384]{1,0:T(8,128)S(1)}, u32[]{:S(2)}, u32[]{:S(2)}) collective-permute-start(f32[144,384]{1,0:T(8,128)S(1)} %get-tuple-element.95), channel_id=1, source_target_pairs={{0,64},{16,80},{32,96},{48,112},{64,0},{80,16},{96,32},{112,48},{1... | collective-permute-start | bytes 663560 | tf_op jit(solution)/shard_map/ppermute | solution.py:21
  48.7 4.6 %collective-permute-start.13 = (f32[72,384]{1,0:T(8,128)S(1)}, f32[72,384]{1,0:T(8,128)S(1)}, u32[]{:S(2)}, u32[]{:S(2)}) collective-permute-start(f32[72,384]{1,0:T(8,128)S(1)} %get-tuple-element.98.a_ref), channel_id=1, source_target_pairs={{0,16},{16,0},{32,48},{48,32},{64,80},{80,64},{96,112},{112,96},{1... | collective-permute-start | bytes 331784 | tf_op jit(solution)/shard_map/ppermute | solution.py:29
  54.7 1.6 %collective-permute-done.12 = f32[144,384]{1,0:T(8,128)S(1)} collective-permute-done((f32[144,384]{1,0:T(8,128)S(1)}, f32[144,384]{1,0:T(8,128)S(1)}, u32[]{:S(2)}, u32[]{:S(2)}) %collective-permute-start.12) | collective-permute-done | bytes 221216 | tf_op jit(solution)/shard_map/ppermute | solution.py:21
  56.5 3.0 %shard_map.48 = f32[72,768]{1,0:T(8,128)} custom-call(s32[12]{0:T(128)S(1)} %stack.51.facts_ref, s32[384,3]{1,0:T(8,128)S(1)} %bitcast.55, f32[72,768]{1,0:T(8,128)S(1)} %bitcast.54, f32[72,384]{1,0:T(8,128)S(1)} %get-tuple-element.98.a_ref, f32[72,384]{1,0:T(8,128)S(1)} %collective-permute-done.13.other_ref, f32[72,384]{1,0:T(8,128)S(1)} %get-tuple-element.97.b_ref, ...), custom_call_target="tpu_custom_call" | custom-call | flops 382205952 | bytes 1048576 | tf_op jit(solution)/shard_map/pallas_call | solution.py:366
  60.9 1.8 %collective-permute-start.18 = (f32[3,48,384]{2,1,0:T(8,128)S(1)}, f32[3,48,384]{2,1,0:T(8,128)S(1)}, u32[]{:S(2)}, u32[]{:S(2)}) collective-permute-start(f32[3,48,384]{2,1,0:T(8,128)S(1)} %bitcast.58), channel_id=1, source_target_pairs={{0,32},{16,48},{32,64},{48,80},{64,96},{80,112},{96,0},{112,16},{1... | collective-permute-start | bytes 663560 | tf_op jit(solution)/shard_map/ppermute | solution.py:21
  62.7 2.7 %collective-permute-start.19 = (f32[3,48,384]{2,1,0:T(8,128)S(1)}, f32[3,48,384]{2,1,0:T(8,128)}, u32[]{:S(2)}, u32[]{:S(2)}) collective-permute-start(f32[3,48,384]{2,1,0:T(8,128)S(1)} %bitcast.59), channel_id=1, source_target_pairs={{0,64},{16,80},{32,96},{48,112},{64,0},{80,16},{96,32},{112,48},{1... | collective-permute-start | bytes 663560 | tf_op jit(solution)/shard_map/ppermute | solution.py:21
  65.5 2.0 %collective-permute-start.20 = (f32[3,48,384]{2,1,0:T(8,128)S(1)}, f32[3,48,384]{2,1,0:T(8,128)}, u32[]{:S(2)}, u32[]{:S(2)}) collective-permute-start(f32[3,48,384]{2,1,0:T(8,128)S(1)} %bitcast.60), channel_id=1, source_target_pairs={{0,96},{16,112},{32,0},{48,16},{64,32},{80,48},{96,64},{112,80},{1... | collective-permute-start | bytes 663560 | tf_op jit(solution)/shard_map/ppermute | solution.py:21
  67.4 4.9 %collective-permute-start.16 = (f32[2,48,384]{2,1,0:T(8,128)S(1)}, f32[2,48,384]{2,1,0:T(8,128)S(1)}, u32[]{:S(2)}, u32[]{:S(2)}) collective-permute-start(f32[2,48,384]{2,1,0:T(8,128)S(1)} %fusion.5), channel_id=1, source_target_pairs={{0,8},{1,9},{2,10},{16,24},{17,25},{18,26},{32,40},{33,41},{34,42}... | collective-permute-start | bytes 442376 | tf_op jit(solution)/shard_map/ppermute | solution.py:43
  78.3 3.1 %collective-permute-done.21 = f32[2,48,384]{2,1,0:T(8,128)S(1)} collective-permute-done((f32[2,48,384]{2,1,0:T(8,128)S(1)}, f32[2,48,384]{2,1,0:T(8,128)S(1)}, u32[]{:S(2)}, u32[]{:S(2)}) %collective-permute-start.21) | collective-permute-done | bytes 147488 | tf_op jit(solution)/shard_map/ppermute | solution.py:37
  82.8 1.8 %collective-permute-done.23 = f32[2,48,384]{2,1,0:T(8,128)S(1)} collective-permute-done((f32[2,48,384]{2,1,0:T(8,128)S(1)}, f32[2,48,384]{2,1,0:T(8,128)S(1)}, u32[]{:S(2)}, u32[]{:S(2)}) %collective-permute-start.23) | collective-permute-done | bytes 147488 | tf_op jit(solution)/shard_map/ppermute | solution.py:37
  85.9 4.2 %collective-permute-start.25 = (f32[3,2,48,384]{3,2,1,0:T(8,128)S(1)}, f32[3,2,48,384]{3,2,1,0:T(8,128)S(1)}, u32[]{:S(2)}, u32[]{:S(2)}) collective-permute-start(f32[3,2,48,384]{3,2,1,0:T(8,128)S(1)} %slice.61.refs_0_), channel_id=1, source_target_pairs={{0,64},{16,80},{32,96},{48,112},{64,0},{80,16},{96,32},{112,48},{1... | collective-permute-start | bytes 1327112 | tf_op jit(solution)/shard_map/ppermute | solution.py:21
  90.1 2.0 %collective-permute-start.26 = (f32[3,2,48,384]{3,2,1,0:T(8,128)S(1)}, f32[3,2,48,384]{3,2,1,0:T(8,128)S(1)}, u32[]{:S(2)}, u32[]{:S(2)}) collective-permute-start(f32[3,2,48,384]{3,2,1,0:T(8,128)S(1)} %slice.61.refs_0_), channel_id=1, source_target_pairs={{0,96},{16,112},{32,0},{48,16},{64,32},{80,48},{96,64},{112,80},{1... | collective-permute-start | bytes 1327112 | tf_op jit(solution)/shard_map/ppermute | solution.py:21
  92.1 3.2 %collective-permute-start.31 = (f32[3,48,384]{2,1,0:T(8,128)S(1)}, f32[3,48,384]{2,1,0:T(8,128)}, u32[]{:S(2)}, u32[]{:S(2)}) collective-permute-start(f32[3,48,384]{2,1,0:T(8,128)S(1)} %bitcast.62), channel_id=1, source_target_pairs={{0,16},{16,0},{32,48},{48,32},{64,80},{80,64},{96,112},{112,96},{1... | collective-permute-start | bytes 663560 | tf_op jit(solution)/shard_map/ppermute | solution.py:29
  95.3 6.9 %shard_map.49.here_ref = f32[768,384]{1,0:T(8,128)} custom-call(s32[12]{0:T(128)} %copy-done.6, s32[3,384]{1,0:T(4,128)} %pivots_ref.3, f32[768,384]{1,0:T(8,128)} %bitcast.48, f32[8,384,384]{2,1,0:T(8,128)} %bitcast.65), custom_call_target="tpu_custom_call" | custom-call | flops 2038431744 | bytes 5242880 | tf_op jit(solution)/shard_map/pallas_call | solution.py:393
  103.2 6.2 %collective-permute-done.26.refs_3_ = f32[3,2,48,384]{3,2,1,0:T(8,128)S(1)} collective-permute-done((f32[3,2,48,384]{3,2,1,0:T(8,128)S(1)}, f32[3,2,48,384]{3,2,1,0:T(8,128)S(1)}, u32[]{:S(2)}, u32[]{:S(2)}) %collective-permute-start.26) | collective-permute-done | bytes 442400 | tf_op jit(solution)/shard_map/ppermute | solution.py:21
  111.8 2.4 %collective-permute-done.34.refs_15_ = f32[3,48,384]{2,1,0:T(8,128)S(1)} collective-permute-done((f32[3,48,384]{2,1,0:T(8,128)}, f32[3,48,384]{2,1,0:T(8,128)S(1)}, u32[]{:S(2)}, u32[]{:S(2)}) %collective-permute-start.34) | collective-permute-done | bytes 221216 | tf_op jit(solution)/shard_map/ppermute | solution.py:29
  116.1 15.6 %shard_map.50 = (f32[1152,384]{1,0:T(8,128)}, f32[384,384]{1,0:T(8,128)}) custom-call(s32[12]{0:T(128)} %copy-done.6, f32[3,2,48,384]{3,2,1,0:T(8,128)} %copy-done.12, f32[3,2,48,384]{3,2,1,0:T(8,128)} %copy-done.16, f32[3,2,48,384]{3,2,1,0:T(8,128)} %copy-done.17, f32[3,2,48,384]{3,2,1,0:T(8,128)} %copy-done.18, f32[3,2,48,384]{3,2,1,0:T(8,128)} %copy-done.19, ...), custom_call_target="tpu_custom_call" | custom-call | flops 6794772480 | bytes 11534336 | tf_op jit(solution)/shard_map/pallas_call | solution.py:405
  131.7 8.0 %shard_map.51 = f32[768,384]{1,0:T(8,128)} custom-call(s32[12]{0:T(128)} %copy-done.6, f32[1152,768]{1,0:T(8,128)} %all-gather.5.cloned.1.call-done.panel_ref, f32[1152,384]{1,0:T(8,128)} %get-tuple-element.86.basis_ref, f32[768,384]{1,0:T(8,128)} %shard_map.49.here_ref, f32[384,384]{1,0:T(8,128)} %get-tuple-element.88.head_ref), custom_call_target="tpu_custom_call" | custom-call | flops 2038431744 | bytes 8388608 | tf_op jit(solution)/shard_map/pallas_call | solution.py:419
  (134 shorter events, 32.9 us)
Async XLA Ops:
  6.5 88.8 %all-gather.7.cloned.1.call-start = ((), (), s32[]{:S(2)}) async-start(), calls=%async_computation.1 | async-start | bytes 5308416 | tf_op jit(solution)/shard_map/all_gather | solution.py:321
  8.6 123.1 %all-gather.5.cloned.1.call-start = ((), (), s32[]{:S(2)}) async-start(), calls=%async_computation | async-start | bytes 3760128 | tf_op jit(solution)/shard_map/all_gather | solution.py:373
  9.0 13.2 %collective-permute-start = (f32[96,768]{0,1:T(8,128)S(1)}, f32[96,768]{0,1:T(8,128)S(1)}, u32[]{:S(2)}, u32[]{:S(2)}) collective-permute-start(f32[96,768]{0,1:T(8,128)S(1)} %get-tuple-element.93), channel_id=1, source_target_pairs={{0,4},{1,5},{2,6},{16,20},{17,21},{18,22},{32,36},{33,37},{34,38},... | collective-permute-start | bytes 884744 | tf_op jit(solution)/shard_map/ppermute | solution.py:43
  12.6 16.2 %collective-permute-start.1 = (f32[96,768]{0,1:T(8,128)S(1)}, f32[96,768]{0,1:T(8,128)S(1)}, u32[]{:S(2)}, u32[]{:S(2)}) collective-permute-start(f32[96,768]{0,1:T(8,128)S(1)} %get-tuple-element.92), channel_id=1, source_target_pairs={{0,8},{1,9},{2,10},{16,24},{17,25},{18,26},{32,40},{33,41},{34,42}... | collective-permute-start | bytes 884744 | tf_op jit(solution)/shard_map/ppermute | solution.py:43
  15.2 13.5 %collective-permute-start.2 = (f32[96,768]{0,1:T(8,128)S(1)}, f32[96,768]{0,1:T(8,128)S(1)}, u32[]{:S(2)}, u32[]{:S(2)}) collective-permute-start(f32[96,768]{0,1:T(8,128)S(1)} %get-tuple-element.91), channel_id=1, source_target_pairs={{0,12},{1,13},{2,14},{16,28},{17,29},{18,30},{32,44},{33,45},{34,4... | collective-permute-start | bytes 884744 | tf_op jit(solution)/shard_map/ppermute | solution.py:43
  28.8 9.5 %collective-permute-start.6 = (f32[576,384]{1,0:T(8,128)}, f32[576,384]{1,0:T(8,128)}, u32[]{:S(2)}, u32[]{:S(2)}) collective-permute-start(f32[576,384]{1,0:T(8,128)} %get-tuple-element.52), channel_id=1, source_target_pairs={{0,16},{16,0},{32,48},{48,32},{64,80},{80,64},{96,112},{112,96},{1... | collective-permute-start | bytes 2654216 | tf_op jit(solution)/shard_map/ppermute | solution.py:29
  38.4 10.2 %collective-permute-start.7 = (f32[72,384]{1,0:T(8,128)S(1)}, f32[72,384]{1,0:T(8,128)S(1)}, u32[]{:S(2)}, u32[]{:S(2)}) collective-permute-start(f32[72,384]{1,0:T(8,128)S(1)} %slice.57), channel_id=1, source_target_pairs={{0,32},{16,48},{32,64},{1,33},{17,49},{33,65},{2,34},{18,50},{34,6... | collective-permute-start | bytes 331784 | tf_op jit(solution)/shard_map/ppermute | solution.py:25
  39.7 8.9 %collective-permute-start.8 = (f32[72,384]{1,0:T(8,128)S(1)}, f32[72,384]{1,0:T(8,128)S(1)}, u32[]{:S(2)}, u32[]{:S(2)}) collective-permute-start(f32[72,384]{1,0:T(8,128)S(1)} %slice.57), channel_id=1, source_target_pairs={{0,64},{16,80},{32,96},{1,65},{17,81},{33,97},{2,66},{18,82},{34,9... | collective-permute-start | bytes 331784 | tf_op jit(solution)/shard_map/ppermute | solution.py:25
  40.4 8.2 %collective-permute-start.9 = (f32[72,384]{1,0:T(8,128)S(1)}, f32[72,384]{1,0:T(8,128)S(1)}, u32[]{:S(2)}, u32[]{:S(2)}) collective-permute-start(f32[72,384]{1,0:T(8,128)S(1)} %slice.57), channel_id=1, source_target_pairs={{0,96},{16,112},{32,0},{1,97},{17,113},{33,1},{2,98},{18,114},{34,... | collective-permute-start | bytes 331784 | tf_op jit(solution)/shard_map/ppermute | solution.py:25
  42.5 12.2 %collective-permute-start.10 = (f32[144,384]{1,0:T(8,128)S(1)}, f32[144,384]{1,0:T(8,128)S(1)}, u32[]{:S(2)}, u32[]{:S(2)}) collective-permute-start(f32[144,384]{1,0:T(8,128)S(1)} %get-tuple-element.96), channel_id=1, source_target_pairs={{0,32},{16,48},{32,64},{48,80},{64,96},{80,112},{96,0},{112,16},{1... | collective-permute-start | bytes 663560 | tf_op jit(solution)/shard_map/ppermute | solution.py:21
  43.8 10.9 %collective-permute-start.11 = (f32[144,384]{1,0:T(8,128)S(1)}, f32[144,384]{1,0:T(8,128)S(1)}, u32[]{:S(2)}, u32[]{:S(2)}) collective-permute-start(f32[144,384]{1,0:T(8,128)S(1)} %get-tuple-element.95), channel_id=1, source_target_pairs={{0,64},{16,80},{32,96},{48,112},{64,0},{80,16},{96,32},{112,48},{1... | collective-permute-start | bytes 663560 | tf_op jit(solution)/shard_map/ppermute | solution.py:21
  48.6 7.7 %collective-permute-start.12 = (f32[144,384]{1,0:T(8,128)S(1)}, f32[144,384]{1,0:T(8,128)S(1)}, u32[]{:S(2)}, u32[]{:S(2)}) collective-permute-start(f32[144,384]{1,0:T(8,128)S(1)} %get-tuple-element.94), channel_id=1, source_target_pairs={{0,96},{16,112},{32,0},{48,16},{64,32},{80,48},{96,64},{112,80},{1... | collective-permute-start | bytes 663560 | tf_op jit(solution)/shard_map/ppermute | solution.py:21
  48.7 7.6 %collective-permute-start.13 = (f32[72,384]{1,0:T(8,128)S(1)}, f32[72,384]{1,0:T(8,128)S(1)}, u32[]{:S(2)}, u32[]{:S(2)}) collective-permute-start(f32[72,384]{1,0:T(8,128)S(1)} %get-tuple-element.98.a_ref), channel_id=1, source_target_pairs={{0,16},{16,0},{32,48},{48,32},{64,80},{80,64},{96,112},{112,96},{1... | collective-permute-start | bytes 331784 | tf_op jit(solution)/shard_map/ppermute | solution.py:29
  59.6 12.7 %collective-permute-start.15 = (f32[2,48,384]{2,1,0:T(8,128)S(1)}, f32[2,48,384]{2,1,0:T(8,128)S(1)}, u32[]{:S(2)}, u32[]{:S(2)}) collective-permute-start(f32[2,48,384]{2,1,0:T(8,128)S(1)} %fusion.5), channel_id=1, source_target_pairs={{0,4},{1,5},{2,6},{16,20},{17,21},{18,22},{32,36},{33,37},{34,38},... | collective-permute-start | bytes 442376 | tf_op jit(solution)/shard_map/ppermute | solution.py:43
  60.9 14.8 %collective-permute-start.18 = (f32[3,48,384]{2,1,0:T(8,128)S(1)}, f32[3,48,384]{2,1,0:T(8,128)S(1)}, u32[]{:S(2)}, u32[]{:S(2)}) collective-permute-start(f32[3,48,384]{2,1,0:T(8,128)S(1)} %bitcast.58), channel_id=1, source_target_pairs={{0,32},{16,48},{32,64},{48,80},{64,96},{80,112},{96,0},{112,16},{1... | collective-permute-start | bytes 663560 | tf_op jit(solution)/shard_map/ppermute | solution.py:21
  62.7 13.0 %collective-permute-start.19 = (f32[3,48,384]{2,1,0:T(8,128)S(1)}, f32[3,48,384]{2,1,0:T(8,128)}, u32[]{:S(2)}, u32[]{:S(2)}) collective-permute-start(f32[3,48,384]{2,1,0:T(8,128)S(1)} %bitcast.59), channel_id=1, source_target_pairs={{0,64},{16,80},{32,96},{48,112},{64,0},{80,16},{96,32},{112,48},{1... | collective-permute-start | bytes 663560 | tf_op jit(solution)/shard_map/ppermute | solution.py:21
  65.5 10.3 %collective-permute-start.20 = (f32[3,48,384]{2,1,0:T(8,128)S(1)}, f32[3,48,384]{2,1,0:T(8,128)}, u32[]{:S(2)}, u32[]{:S(2)}) collective-permute-start(f32[3,48,384]{2,1,0:T(8,128)S(1)} %bitcast.60), channel_id=1, source_target_pairs={{0,96},{16,112},{32,0},{48,16},{64,32},{80,48},{96,64},{112,80},{1... | collective-permute-start | bytes 663560 | tf_op jit(solution)/shard_map/ppermute | solution.py:21
  67.4 7.0 %collective-permute-start.16 = (f32[2,48,384]{2,1,0:T(8,128)S(1)}, f32[2,48,384]{2,1,0:T(8,128)S(1)}, u32[]{:S(2)}, u32[]{:S(2)}) collective-permute-start(f32[2,48,384]{2,1,0:T(8,128)S(1)} %fusion.5), channel_id=1, source_target_pairs={{0,8},{1,9},{2,10},{16,24},{17,25},{18,26},{32,40},{33,41},{34,42}... | collective-permute-start | bytes 442376 | tf_op jit(solution)/shard_map/ppermute | solution.py:43
  84.7 17.5 %collective-permute-start.24 = (f32[3,2,48,384]{3,2,1,0:T(8,128)S(1)}, f32[3,2,48,384]{3,2,1,0:T(8,128)S(1)}, u32[]{:S(2)}, u32[]{:S(2)}) collective-permute-start(f32[3,2,48,384]{3,2,1,0:T(8,128)S(1)} %slice.61.refs_0_), channel_id=1, source_target_pairs={{0,32},{16,48},{32,64},{48,80},{64,96},{80,112},{96,0},{112,16},{1... | collective-permute-start | bytes 1327112 | tf_op jit(solution)/shard_map/ppermute | solution.py:21
  85.9 17.3 %collective-permute-start.25 = (f32[3,2,48,384]{3,2,1,0:T(8,128)S(1)}, f32[3,2,48,384]{3,2,1,0:T(8,128)S(1)}, u32[]{:S(2)}, u32[]{:S(2)}) collective-permute-start(f32[3,2,48,384]{3,2,1,0:T(8,128)S(1)} %slice.61.refs_0_), channel_id=1, source_target_pairs={{0,64},{16,80},{32,96},{48,112},{64,0},{80,16},{96,32},{112,48},{1... | collective-permute-start | bytes 1327112 | tf_op jit(solution)/shard_map/ppermute | solution.py:21
  90.1 19.3 %collective-permute-start.26 = (f32[3,2,48,384]{3,2,1,0:T(8,128)S(1)}, f32[3,2,48,384]{3,2,1,0:T(8,128)S(1)}, u32[]{:S(2)}, u32[]{:S(2)}) collective-permute-start(f32[3,2,48,384]{3,2,1,0:T(8,128)S(1)} %slice.61.refs_0_), channel_id=1, source_target_pairs={{0,96},{16,112},{32,0},{48,16},{64,32},{80,48},{96,64},{112,80},{1... | collective-permute-start | bytes 1327112 | tf_op jit(solution)/shard_map/ppermute | solution.py:21
  92.1 18.7 %collective-permute-start.31 = (f32[3,48,384]{2,1,0:T(8,128)S(1)}, f32[3,48,384]{2,1,0:T(8,128)}, u32[]{:S(2)}, u32[]{:S(2)}) collective-permute-start(f32[3,48,384]{2,1,0:T(8,128)S(1)} %bitcast.62), channel_id=1, source_target_pairs={{0,16},{16,0},{32,48},{48,32},{64,80},{80,64},{96,112},{112,96},{1... | collective-permute-start | bytes 663560 | tf_op jit(solution)/shard_map/ppermute | solution.py:29
  95.3 15.9 %collective-permute-start.32 = (f32[3,48,384]{2,1,0:T(8,128)S(1)}, f32[3,48,384]{2,1,0:T(8,128)}, u32[]{:S(2)}, u32[]{:S(2)}) collective-permute-start(f32[3,48,384]{2,1,0:T(8,128)S(1)} %collective-permute-done.18.refs_9_), channel_id=1, source_target_pairs={{0,16},{16,0},{32,48},{48,32},{64,80},{80,64},{96,112},{112,96},{1... | collective-permute-start | bytes 663560 | tf_op jit(solution)/shard_map/ppermute | solution.py:29
  102.2 9.1 %collective-permute-start.33 = (f32[3,48,384]{2,1,0:T(8,128)}, f32[3,48,384]{2,1,0:T(8,128)S(1)}, u32[]{:S(2)}, u32[]{:S(2)}) collective-permute-start(f32[3,48,384]{2,1,0:T(8,128)} %collective-permute-done.19.refs_10_), channel_id=1, source_target_pairs={{0,16},{16,0},{32,48},{48,32},{64,80},{80,64},{96,112},{112,96},{1... | collective-permute-start | bytes 663560 | tf_op jit(solution)/shard_map/ppermute | solution.py:29
  (39 other events, 266.7 us)
Sparse Core Ops, SparseCore 0:
  9.0 35.9 all-gather.6
  59.6 58.0 all-gather.4
where the time goes:
time: 149 us; the launch traced here: 147 us
  starting transfers between devices  57.4 us (39%)
  Pallas kernels  39.4 us (26%)
  waiting for transfers between devices  25.4 us (17%)
  between operations  14.1 us (9%)
  local copies, waits for them, and re-layouts  7.27 us (5%)
  other arithmetic  3.04 us (2%)
    ppermute x9, starting transfers between devices, x_shift(): lax.ppermute(v, 'prow', [(p, (p + 2 * k) % PROWS) for p in range(PROWS)])  20 us
    pallas_call x1, Pallas kernels, on_device(): pl.pallas_call(factor_kernel, out_shape=(shape(TOP, W), shape(W, W)), in_...  15.6 us
    ppermute x6, starting transfers between devices, from_z0(): return lax.ppermute(v, 'pcol', [(y, k * NY + y) for y in range(STEPS)])  15.2 us
    ppermute x10, starting transfers between devices, sibling(): return lax.ppermute(v, 'prow', [(p, p ^ 1) for p in range(PROWS)])  12.6 us
    ppermute x6, waiting for transfers between devices, from_z0(): return lax.ppermute(v, 'pcol', [(y, k * NY + y) for y in range(STEPS)])  8.44 us
    pallas_call x1, Pallas kernels, on_device(): pl.pallas_call(final_kernel, out_shape=shape(ROWS, W), in_specs=[SMEM, HB...  7.98 us
    ppermute x9, waiting for transfers between devices, x_shift(): lax.ppermute(v, 'prow', [(p, (p + 2 * k) % PROWS) for p in range(PROWS)])  7.8 us
    pallas_call x1, Pallas kernels, on_device(): pl.pallas_call(rows_kernel, out_shape=shape(ROWS, W), in_specs=[SMEM, WHO...  6.88 us
  transfers between devices with their start and end apart: 37, of which 11 were waited for; matrix products, arithmetic and copies ran while one was open for 3% of the time, Pallas kernels for 21%

commit v1 on v0

--- a/solution.py
+++ b/solution.py
@@ -21,16 +21,8 @@
     return lax.ppermute(v, "prow", [(p, (p + 2 * k) % PROWS) for p in range(PROWS)])
 
 
-def x_shift_top(v, k):
-    return lax.ppermute(v, "prow", [(p, (p + 2 * k) % PROWS) for p in range(STEPS)])
-
-
 def sibling(v):
     return lax.ppermute(v, "prow", [(p, p ^ 1) for p in range(PROWS)])
-
-
-def to_odd(v):
-    return lax.ppermute(v, "prow", [(p, p + 1) for p in range(0, PROWS, 2)])
 
 
 def y_shift(v, k):
@@ -354,13 +346,13 @@
     strips = placed(cut[:1] + got, [(y - k) % NY for k in range(NY)], 0)[:STEPS]
     strips = strips.reshape(STEPS * COLS, ROWS)
     strip_tops = strips[:, :W]
-    tops_got = [x_shift_top(strip_tops, k) for k in (1, 2, 3)]
+    tops_got = [x_shift(strip_tops, k) for k in (1, 2, 3)]
 
     around = [x_shift(summed[k], k) for k in (1, 2, 3)]
 
     *tops_got, summed = lax.optimization_barrier((*tops_got, summed))
     a, b = tops_by_x(strip_tops, tops_got, x, core)
-    a_other, b_far = sibling(a), to_odd(b)
+    a_other, b_far = sibling(a), sibling(b)
 
     *around, a_other, b_far = lax.optimization_barrier((*around, a_other, b_far))
     strips = pl.pallas_call(
@@ -378,15 +370,16 @@
     twice = jnp.concatenate([parts, parts])
     off = lax.dynamic_slice_in_dim(twice, (y + 1) % STEPS, 2, axis=0)
     got = [from_z0(off, k) for k in (1, 2, 3)]
-    near = [parts] + [x_shift(parts, k) for k in (1, 2, 3)]
-
-    got_near = lax.optimization_barrier((*got, strips, *near))
-    got, strips, near = got_near[:3], got_near[3], list(got_near[4:])
-    near = near + [sibling(v) for v in near]
+
+    *got, strips, early = lax.optimization_barrier((*got, strips, parts))
     spread = jnp.where(z == 0, off, 0.0)
     for v in got:
         spread = spread + v
     line = [spread] + [y_shift(spread, k) for k in (1, 2, 3)]
+    near = [early] + [x_shift(early, k) for k in (1, 2, 3)]
+    line_near = lax.optimization_barrier((*line, *near))
+    line, near = line_near[:NY], list(line_near[NY:])
+    near = near + [sibling(v) for v in near]
     line = placed(line, [(y - k) % NY for k in range(NY)], 0)[:STEPS]
     ring = [line] + [x_shift(line, k) for k in (1, 2, 3)]
 

time: 149 us -> 147 us (0.987); the launches traced: 147 us -> 147 us
  waiting for transfers between devices: 25.4 us -> 33.5 us
  starting transfers between devices: 57.4 us -> 49.5 us
    ppermute x9 -> x12, starting transfers between devices: 20 us -> 12.6 us  [x_shift(): lax.ppermute(v, 'prow', [(p, (p + 2 * k) % PROWS) for p in range(PROWS)])]
    ppermute x9 -> x12, waiting for transfers between devices: 7.8 us -> 13.4 us  [x_shift(): lax.ppermute(v, 'prow', [(p, (p + 2 * k) % PROWS) for p in range(PROWS)])]
    ppermute x4 -> x0, starting transfers between devices: 3.91 us -> none  [the longest x3 2.63 us: x_shift_top(): lax.ppermute(v, 'prow', [(p, (p + 2 * k) % PROWS) for p in range(STEPS)])]
    ppermute x6, waiting for transfers between devices: 6.35 us -> 8.92 us  [y_shift(): lax.ppermute(v, 'pcol', [(z * NY + y, z * NY + (y + k) % NY) for z in ran...]
    ppermute x6, starting transfers between devices: 5.63 us -> 7.63 us  [y_shift(): lax.ppermute(v, 'pcol', [(z * NY + y, z * NY + (y + k) % NY) for z in ran...]
    ppermute x10 -> x11, starting transfers between devices: 12.6 us -> 13.9 us  [sibling(): return lax.ppermute(v, 'prow', [(p, p ^ 1) for p in range(PROWS)])]
  transfers between devices with their start and end apart: 37 -> 37, of which waited for: 11 -> 10; matrix products, arithmetic and copies ran while one was open for 3% -> 3% of each run, Pallas kernels for 21% -> 21%
where the time goes in v1:
time: 147 us
  starting transfers between devices  49.5 us (34%)
  Pallas kernels  39.4 us (27%)
  waiting for transfers between devices  33.5 us (23%)
  between operations  14.1 us (10%)
  local copies, waits for them, and re-layouts  7.31 us (5%)
  other arithmetic  3.04 us (2%)
    pallas_call x1, Pallas kernels, on_device(): pl.pallas_call(factor_kernel, out_shape=(shape(TOP, W), shape(W, W)), in_...  15.7 us
    ppermute x6, starting transfers between devices, from_z0(): return lax.ppermute(v, 'pcol', [(y, k * NY + y) for y in range(STEPS)])  15.3 us
    ppermute x11, starting transfers between devices, sibling(): return lax.ppermute(v, 'prow', [(p, p ^ 1) for p in range(PROWS)])  13.9 us
    ppermute x12, waiting for transfers between devices, x_shift(): lax.ppermute(v, 'prow', [(p, (p + 2 * k) % PROWS) for p in range(PROWS)])  13.4 us
    ppermute x12, starting transfers between devices, x_shift(): lax.ppermute(v, 'prow', [(p, (p + 2 * k) % PROWS) for p in range(PROWS)])  12.6 us
    ppermute x6, waiting for transfers between devices, y_shift(): lax.ppermute(v, 'pcol', [(z * NY + y, z * NY + (y + k) % NY) for z in ran...  8.92 us
    ppermute x6, waiting for transfers between devices, from_z0(): return lax.ppermute(v, 'pcol', [(y, k * NY + y) for y in range(STEPS)])  8.61 us
    pallas_call x1, Pallas kernels, on_device(): pl.pallas_call(final_kernel, out_shape=shape(ROWS, W), in_specs=[SMEM, HB...  7.98 us
  transfers between devices with their start and end apart: 37, of which 10 were waited for; matrix products, arithmetic and copies ran while one was open for 3% of the time, Pallas kernels for 21%

profile of v1, /device:TPU:11, one launch (start us, length us, event | category | flops | bytes accessed | tf_op | source)
XLA Modules:
  0.0 146.8 jit_solution(4536733175328863169)
XLA Ops:
  6.5 2.0 %slice.51 = f32[1,1,384,384]{3,2,1,0:T(8,128)} slice(f32[1,1,768,384]{3,2,1,0:T(8,128)} %param.4), slice={[0:1], [0:1], [0:384], [0:384]} | slice | bytes 1179648 | tf_op jit(solution)/shard_map/slice | solution.py:313
  9.0 3.6 %collective-permute-start = (f32[96,768]{0,1:T(8,128)S(1)}, f32[96,768]{0,1:T(8,128)S(1)}, u32[]{:S(2)}, u32[]{:S(2)}) collective-permute-start(f32[96,768]{0,1:T(8,128)S(1)} %get-tuple-element.101), channel_id=1, source_target_pairs={{0,4},{1,5},{2,6},{16,20},{17,21},{18,22},{32,36},{33,37},{34,38},... | collective-permute-start | bytes 884744 | tf_op jit(solution)/shard_map/ppermute | solution.py:35
  12.6 2.6 %collective-permute-start.1 = (f32[96,768]{0,1:T(8,128)S(1)}, f32[96,768]{0,1:T(8,128)S(1)}, u32[]{:S(2)}, u32[]{:S(2)}) collective-permute-start(f32[96,768]{0,1:T(8,128)S(1)} %get-tuple-element.100), channel_id=1, source_target_pairs={{0,8},{1,9},{2,10},{16,24},{17,25},{18,26},{32,40},{33,41},{34,42}... | collective-permute-start | bytes 884744 | tf_op jit(solution)/shard_map/ppermute | solution.py:35
  16.8 4.5 %shard_map.46 = (f32[576,384]{1,0:T(8,128)S(1)}, f32[576,384]{1,0:T(8,128)}) custom-call(s32[12]{0:T(128)S(1)} %stack.51.facts_ref, s32[3,384]{1,0:T(4,128)S(1)} %copy-done.5, f32[768,384]{1,0:T(8,128)S(1)} %bitcast.50), custom_call_target="tpu_custom_call" | custom-call | flops 2038431744 | bytes 3145728 | tf_op jit(solution)/shard_map/pallas_call | solution.py:315
  22.2 6.5 %collective-permute-done.1 = f32[96,768]{0,1:T(8,128)S(1)} collective-permute-done((f32[96,768]{0,1:T(8,128)S(1)}, f32[96,768]{0,1:T(8,128)S(1)}, u32[]{:S(2)}, u32[]{:S(2)}) %collective-permute-start.1) | collective-permute-done | bytes 294944 | tf_op jit(solution)/shard_map/ppermute | solution.py:35
  40.8 1.9 %collective-permute-start.9 = (f32[72,384]{1,0:T(8,128)S(1)}, f32[72,384]{1,0:T(8,128)S(1)}, u32[]{:S(2)}, u32[]{:S(2)}) collective-permute-start(f32[72,384]{1,0:T(8,128)S(1)} %slice.57), channel_id=1, source_target_pairs={{0,96},{16,112},{32,0},{48,16},{64,32},{80,48},{96,64},{112,80},{1... | collective-permute-start | bytes 331784 | tf_op jit(solution)/shard_map/ppermute | solution.py:21
  44.1 2.7 %collective-permute-start.11 = (f32[144,384]{1,0:T(8,128)S(1)}, f32[144,384]{1,0:T(8,128)S(1)}, u32[]{:S(2)}, u32[]{:S(2)}) collective-permute-start(f32[144,384]{1,0:T(8,128)S(1)} %get-tuple-element.103), channel_id=1, source_target_pairs={{0,64},{16,80},{32,96},{48,112},{64,0},{80,16},{96,32},{112,48},{1... | collective-permute-start | bytes 663560 | tf_op jit(solution)/shard_map/ppermute | solution.py:21
  46.9 3.9 %collective-permute-start.13 = (f32[72,384]{1,0:T(8,128)S(1)}, f32[72,384]{1,0:T(8,128)S(1)}, u32[]{:S(2)}, u32[]{:S(2)}) collective-permute-start(f32[72,384]{1,0:T(8,128)S(1)} %get-tuple-element.106.a_ref), channel_id=1, source_target_pairs={{0,16},{16,0},{32,48},{48,32},{64,80},{80,64},{96,112},{112,96},{1... | collective-permute-start | bytes 331784 | tf_op jit(solution)/shard_map/ppermute | solution.py:25
  51.6 5.3 %collective-permute-done.12 = f32[144,384]{1,0:T(8,128)S(1)} collective-permute-done((f32[144,384]{1,0:T(8,128)S(1)}, f32[144,384]{1,0:T(8,128)S(1)}, u32[]{:S(2)}, u32[]{:S(2)}) %collective-permute-start.12) | collective-permute-done | bytes 221216 | tf_op jit(solution)/shard_map/ppermute | solution.py:21
  57.0 3.0 %shard_map.48 = f32[72,768]{1,0:T(8,128)} custom-call(s32[12]{0:T(128)S(1)} %stack.51.facts_ref, s32[384,3]{1,0:T(8,128)S(1)} %bitcast.55, f32[72,768]{1,0:T(8,128)S(1)} %bitcast.54, f32[72,384]{1,0:T(8,128)S(1)} %get-tuple-element.106.a_ref, f32[72,384]{1,0:T(8,128)S(1)} %collective-permute-done.13.other_ref, f32[72,384]{1,0:T(8,128)S(1)} %get-tuple-element.105.b_ref, ...), custom_call_target="tpu_custom_call" | custom-call | flops 382205952 | bytes 1048576 | tf_op jit(solution)/shard_map/pallas_call | solution.py:358
  60.1 2.9 %collective-permute-start.15 = (f32[2,48,384]{2,1,0:T(8,128)S(1)}, f32[2,48,384]{2,1,0:T(8,128)S(1)}, u32[]{:S(2)}, u32[]{:S(2)}) collective-permute-start(f32[2,48,384]{2,1,0:T(8,128)S(1)} %fusion.5), channel_id=1, source_target_pairs={{0,4},{1,5},{2,6},{16,20},{17,21},{18,22},{32,36},{33,37},{34,38},... | collective-permute-start | bytes 442376 | tf_op jit(solution)/shard_map/ppermute | solution.py:35
  63.0 3.5 %collective-permute-start.16 = (f32[2,48,384]{2,1,0:T(8,128)S(1)}, f32[2,48,384]{2,1,0:T(8,128)S(1)}, u32[]{:S(2)}, u32[]{:S(2)}) collective-permute-start(f32[2,48,384]{2,1,0:T(8,128)S(1)} %fusion.5), channel_id=1, source_target_pairs={{0,8},{1,9},{2,10},{16,24},{17,25},{18,26},{32,40},{33,41},{34,42}... | collective-permute-start | bytes 442376 | tf_op jit(solution)/shard_map/ppermute | solution.py:35
  70.0 1.8 %collective-permute-start.18 = (f32[2,48,384]{2,1,0:T(8,128)S(1)}, f32[2,48,384]{2,1,0:T(8,128)S(1)}, u32[]{:S(2)}, u32[]{:S(2)}) collective-permute-start(f32[2,48,384]{2,1,0:T(8,128)S(1)} %add_add_fusion), channel_id=1, source_target_pairs={{0,1},{1,2},{2,3},{3,0},{4,5},{5,6},{6,7},{7,4},{8,9},{9,10},{10,1... | collective-permute-start | bytes 442376 | tf_op jit(solution)/shard_map/ppermute | solution.py:29
  71.8 2.0 %collective-permute-start.22 = (f32[3,48,384]{2,1,0:T(8,128)S(1)}, f32[3,48,384]{2,1,0:T(8,128)}, u32[]{:S(2)}, u32[]{:S(2)}) collective-permute-start(f32[3,48,384]{2,1,0:T(8,128)S(1)} %bitcast.60), channel_id=1, source_target_pairs={{0,64},{16,80},{32,96},{48,112},{64,0},{80,16},{96,32},{112,48},{1... | collective-permute-start | bytes 663560 | tf_op jit(solution)/shard_map/ppermute | solution.py:21
  73.9 2.1 %collective-permute-start.23 = (f32[3,48,384]{2,1,0:T(8,128)S(1)}, f32[3,48,384]{2,1,0:T(8,128)}, u32[]{:S(2)}, u32[]{:S(2)}) collective-permute-start(f32[3,48,384]{2,1,0:T(8,128)S(1)} %bitcast.61), channel_id=1, source_target_pairs={{0,96},{16,112},{32,0},{48,16},{64,32},{80,48},{96,64},{112,80},{1... | collective-permute-start | bytes 663560 | tf_op jit(solution)/shard_map/ppermute | solution.py:21
  75.9 2.6 %collective-permute-start.19 = (f32[2,48,384]{2,1,0:T(8,128)S(1)}, f32[2,48,384]{2,1,0:T(8,128)S(1)}, u32[]{:S(2)}, u32[]{:S(2)}) collective-permute-start(f32[2,48,384]{2,1,0:T(8,128)S(1)} %add_add_fusion), channel_id=1, source_target_pairs={{0,2},{1,3},{2,0},{3,1},{4,6},{5,7},{6,4},{7,5},{8,10},{9,11},{10,... | collective-permute-start | bytes 442376 | tf_op jit(solution)/shard_map/ppermute | solution.py:29
  78.5 3.6 %collective-permute-done.19 = f32[2,48,384]{2,1,0:T(8,128)S(1)} collective-permute-done((f32[2,48,384]{2,1,0:T(8,128)S(1)}, f32[2,48,384]{2,1,0:T(8,128)S(1)}, u32[]{:S(2)}, u32[]{:S(2)}) %collective-permute-start.19) | collective-permute-done | bytes 147488 | tf_op jit(solution)/shard_map/ppermute | solution.py:29
  82.1 5.3 %collective-permute-done.20 = f32[2,48,384]{2,1,0:T(8,128)S(1)} collective-permute-done((f32[2,48,384]{2,1,0:T(8,128)S(1)}, f32[2,48,384]{2,1,0:T(8,128)S(1)}, u32[]{:S(2)}, u32[]{:S(2)}) %collective-permute-start.20) | collective-permute-done | bytes 147488 | tf_op jit(solution)/shard_map/ppermute | solution.py:29
  89.2 5.4 %collective-permute-start.31 = (f32[3,48,384]{2,1,0:T(8,128)S(1)}, f32[3,48,384]{2,1,0:T(8,128)}, u32[]{:S(2)}, u32[]{:S(2)}) collective-permute-start(f32[3,48,384]{2,1,0:T(8,128)S(1)} %bitcast.62), channel_id=1, source_target_pairs={{0,16},{16,0},{32,48},{48,32},{64,80},{80,64},{96,112},{112,96},{1... | collective-permute-start | bytes 663560 | tf_op jit(solution)/shard_map/ppermute | solution.py:25
  94.6 6.9 %shard_map.49.here_ref = f32[768,384]{1,0:T(8,128)} custom-call(s32[12]{0:T(128)} %copy-done.6, s32[3,384]{1,0:T(4,128)} %pivots_ref.3, f32[768,384]{1,0:T(8,128)} %bitcast.48, f32[8,384,384]{2,1,0:T(8,128)} %bitcast.65), custom_call_target="tpu_custom_call" | custom-call | flops 2038431744 | bytes 5242880 | tf_op jit(solution)/shard_map/pallas_call | solution.py:386
  102.6 7.5 %collective-permute-done.26.refs_3_ = f32[3,2,48,384]{3,2,1,0:T(8,128)S(1)} collective-permute-done((f32[3,2,48,384]{3,2,1,0:T(8,128)S(1)}, f32[3,2,48,384]{3,2,1,0:T(8,128)S(1)}, u32[]{:S(2)}, u32[]{:S(2)}) %collective-permute-start.26) | collective-permute-done | bytes 442400 | tf_op jit(solution)/shard_map/ppermute | solution.py:21
  112.0 2.4 %collective-permute-done.34.refs_15_ = f32[3,48,384]{2,1,0:T(8,128)S(1)} collective-permute-done((f32[3,48,384]{2,1,0:T(8,128)}, f32[3,48,384]{2,1,0:T(8,128)S(1)}, u32[]{:S(2)}, u32[]{:S(2)}) %collective-permute-start.34) | collective-permute-done | bytes 221216 | tf_op jit(solution)/shard_map/ppermute | solution.py:25
  116.3 15.7 %shard_map.50 = (f32[1152,384]{1,0:T(8,128)}, f32[384,384]{1,0:T(8,128)}) custom-call(s32[12]{0:T(128)} %copy-done.6, f32[3,2,48,384]{3,2,1,0:T(8,128)} %copy-done.12, f32[3,2,48,384]{3,2,1,0:T(8,128)} %copy-done.16, f32[3,2,48,384]{3,2,1,0:T(8,128)} %copy-done.17, f32[3,2,48,384]{3,2,1,0:T(8,128)} %copy-done.18, f32[3,2,48,384]{3,2,1,0:T(8,128)} %copy-done.19, ...), custom_call_target="tpu_custom_call" | custom-call | flops 6794772480 | bytes 11534336 | tf_op jit(solution)/shard_map/pallas_call | solution.py:398
  132.0 8.0 %shard_map.51 = f32[768,384]{1,0:T(8,128)} custom-call(s32[12]{0:T(128)} %copy-done.6, f32[1152,768]{1,0:T(8,128)} %all-gather.5.cloned.1.call-done.panel_ref, f32[1152,384]{1,0:T(8,128)} %get-tuple-element.96.basis_ref, f32[768,384]{1,0:T(8,128)} %shard_map.49.here_ref, f32[384,384]{1,0:T(8,128)} %get-tuple-element.98.head_ref), custom_call_target="tpu_custom_call" | custom-call | flops 2038431744 | bytes 8388608 | tf_op jit(solution)/shard_map/pallas_call | solution.py:412
  (135 shorter events, 27.1 us)
Async XLA Ops:
  6.5 88.1 %all-gather.7.cloned.1.call-start = ((), (), s32[]{:S(2)}) async-start(), calls=%async_computation.1 | async-start | bytes 5308416 | tf_op jit(solution)/shard_map/all_gather | solution.py:313
  8.6 123.4 %all-gather.5.cloned.1.call-start = ((), (), s32[]{:S(2)}) async-start(), calls=%async_computation | async-start | bytes 3760128 | tf_op jit(solution)/shard_map/all_gather | solution.py:365
  9.0 13.2 %collective-permute-start = (f32[96,768]{0,1:T(8,128)S(1)}, f32[96,768]{0,1:T(8,128)S(1)}, u32[]{:S(2)}, u32[]{:S(2)}) collective-permute-start(f32[96,768]{0,1:T(8,128)S(1)} %get-tuple-element.101), channel_id=1, source_target_pairs={{0,4},{1,5},{2,6},{16,20},{17,21},{18,22},{32,36},{33,37},{34,38},... | collective-permute-start | bytes 884744 | tf_op jit(solution)/shard_map/ppermute | solution.py:35
  12.6 16.2 %collective-permute-start.1 = (f32[96,768]{0,1:T(8,128)S(1)}, f32[96,768]{0,1:T(8,128)S(1)}, u32[]{:S(2)}, u32[]{:S(2)}) collective-permute-start(f32[96,768]{0,1:T(8,128)S(1)} %get-tuple-element.100), channel_id=1, source_target_pairs={{0,8},{1,9},{2,10},{16,24},{17,25},{18,26},{32,40},{33,41},{34,42}... | collective-permute-start | bytes 884744 | tf_op jit(solution)/shard_map/ppermute | solution.py:35
  15.2 13.5 %collective-permute-start.2 = (f32[96,768]{0,1:T(8,128)S(1)}, f32[96,768]{0,1:T(8,128)S(1)}, u32[]{:S(2)}, u32[]{:S(2)}) collective-permute-start(f32[96,768]{0,1:T(8,128)S(1)} %get-tuple-element.99), channel_id=1, source_target_pairs={{0,12},{1,13},{2,14},{16,28},{17,29},{18,30},{32,44},{33,45},{34,4... | collective-permute-start | bytes 884744 | tf_op jit(solution)/shard_map/ppermute | solution.py:35
  28.8 9.5 %collective-permute-start.6 = (f32[576,384]{1,0:T(8,128)}, f32[576,384]{1,0:T(8,128)}, u32[]{:S(2)}, u32[]{:S(2)}) collective-permute-start(f32[576,384]{1,0:T(8,128)} %get-tuple-element.57), channel_id=1, source_target_pairs={{0,16},{16,0},{32,48},{48,32},{64,80},{80,64},{96,112},{112,96},{1... | collective-permute-start | bytes 2654216 | tf_op jit(solution)/shard_map/ppermute | solution.py:25
  38.4 8.4 %collective-permute-start.7 = (f32[72,384]{1,0:T(8,128)S(1)}, f32[72,384]{1,0:T(8,128)S(1)}, u32[]{:S(2)}, u32[]{:S(2)}) collective-permute-start(f32[72,384]{1,0:T(8,128)S(1)} %slice.57), channel_id=1, source_target_pairs={{0,32},{16,48},{32,64},{48,80},{64,96},{80,112},{96,0},{112,16},{1... | collective-permute-start | bytes 331784 | tf_op jit(solution)/shard_map/ppermute | solution.py:21
  39.7 7.1 %collective-permute-start.8 = (f32[72,384]{1,0:T(8,128)S(1)}, f32[72,384]{1,0:T(8,128)S(1)}, u32[]{:S(2)}, u32[]{:S(2)}) collective-permute-start(f32[72,384]{1,0:T(8,128)S(1)} %slice.57), channel_id=1, source_target_pairs={{0,64},{16,80},{32,96},{48,112},{64,0},{80,16},{96,32},{112,48},{1... | collective-permute-start | bytes 331784 | tf_op jit(solution)/shard_map/ppermute | solution.py:21
  44.1 7.0 %collective-permute-start.10 = (f32[144,384]{1,0:T(8,128)S(1)}, f32[144,384]{1,0:T(8,128)S(1)}, u32[]{:S(2)}, u32[]{:S(2)}) collective-permute-start(f32[144,384]{1,0:T(8,128)S(1)} %get-tuple-element.104), channel_id=1, source_target_pairs={{0,32},{16,48},{32,64},{48,80},{64,96},{80,112},{96,0},{112,16},{1... | collective-permute-start | bytes 663560 | tf_op jit(solution)/shard_map/ppermute | solution.py:21
  44.1 7.5 %collective-permute-start.11 = (f32[144,384]{1,0:T(8,128)S(1)}, f32[144,384]{1,0:T(8,128)S(1)}, u32[]{:S(2)}, u32[]{:S(2)}) collective-permute-start(f32[144,384]{1,0:T(8,128)S(1)} %get-tuple-element.103), channel_id=1, source_target_pairs={{0,64},{16,80},{32,96},{48,112},{64,0},{80,16},{96,32},{112,48},{1... | collective-permute-start | bytes 663560 | tf_op jit(solution)/shard_map/ppermute | solution.py:21
  46.8 10.1 %collective-permute-start.12 = (f32[144,384]{1,0:T(8,128)S(1)}, f32[144,384]{1,0:T(8,128)S(1)}, u32[]{:S(2)}, u32[]{:S(2)}) collective-permute-start(f32[144,384]{1,0:T(8,128)S(1)} %get-tuple-element.102), channel_id=1, source_target_pairs={{0,96},{16,112},{32,0},{48,16},{64,32},{80,48},{96,64},{112,80},{1... | collective-permute-start | bytes 663560 | tf_op jit(solution)/shard_map/ppermute | solution.py:21
  46.9 10.0 %collective-permute-start.13 = (f32[72,384]{1,0:T(8,128)S(1)}, f32[72,384]{1,0:T(8,128)S(1)}, u32[]{:S(2)}, u32[]{:S(2)}) collective-permute-start(f32[72,384]{1,0:T(8,128)S(1)} %get-tuple-element.106.a_ref), channel_id=1, source_target_pairs={{0,16},{16,0},{32,48},{48,32},{64,80},{80,64},{96,112},{112,96},{1... | collective-permute-start | bytes 331784 | tf_op jit(solution)/shard_map/ppermute | solution.py:25
  60.1 7.8 %collective-permute-start.15 = (f32[2,48,384]{2,1,0:T(8,128)S(1)}, f32[2,48,384]{2,1,0:T(8,128)S(1)}, u32[]{:S(2)}, u32[]{:S(2)}) collective-permute-start(f32[2,48,384]{2,1,0:T(8,128)S(1)} %fusion.5), channel_id=1, source_target_pairs={{0,4},{1,5},{2,6},{16,20},{17,21},{18,22},{32,36},{33,37},{34,38},... | collective-permute-start | bytes 442376 | tf_op jit(solution)/shard_map/ppermute | solution.py:35
  70.0 8.5 %collective-permute-start.18 = (f32[2,48,384]{2,1,0:T(8,128)S(1)}, f32[2,48,384]{2,1,0:T(8,128)S(1)}, u32[]{:S(2)}, u32[]{:S(2)}) collective-permute-start(f32[2,48,384]{2,1,0:T(8,128)S(1)} %add_add_fusion), channel_id=1, source_target_pairs={{0,1},{1,2},{2,3},{3,0},{4,5},{5,6},{6,7},{7,4},{8,9},{9,10},{10,1... | collective-permute-start | bytes 442376 | tf_op jit(solution)/shard_map/ppermute | solution.py:29
  71.8 15.6 %collective-permute-start.21 = (f32[3,48,384]{2,1,0:T(8,128)S(1)}, f32[3,48,384]{2,1,0:T(8,128)S(1)}, u32[]{:S(2)}, u32[]{:S(2)}) collective-permute-start(f32[3,48,384]{2,1,0:T(8,128)S(1)} %bitcast.59), channel_id=1, source_target_pairs={{0,32},{16,48},{32,64},{48,80},{64,96},{80,112},{96,0},{112,16},{1... | collective-permute-start | bytes 663560 | tf_op jit(solution)/shard_map/ppermute | solution.py:21
  71.8 15.6 %collective-permute-start.22 = (f32[3,48,384]{2,1,0:T(8,128)S(1)}, f32[3,48,384]{2,1,0:T(8,128)}, u32[]{:S(2)}, u32[]{:S(2)}) collective-permute-start(f32[3,48,384]{2,1,0:T(8,128)S(1)} %bitcast.60), channel_id=1, source_target_pairs={{0,64},{16,80},{32,96},{48,112},{64,0},{80,16},{96,32},{112,48},{1... | collective-permute-start | bytes 663560 | tf_op jit(solution)/shard_map/ppermute | solution.py:21
  73.9 13.6 %collective-permute-start.23 = (f32[3,48,384]{2,1,0:T(8,128)S(1)}, f32[3,48,384]{2,1,0:T(8,128)}, u32[]{:S(2)}, u32[]{:S(2)}) collective-permute-start(f32[3,48,384]{2,1,0:T(8,128)S(1)} %bitcast.61), channel_id=1, source_target_pairs={{0,96},{16,112},{32,0},{48,16},{64,32},{80,48},{96,64},{112,80},{1... | collective-permute-start | bytes 663560 | tf_op jit(solution)/shard_map/ppermute | solution.py:21
  78.5 8.9 %collective-permute-start.20 = (f32[2,48,384]{2,1,0:T(8,128)S(1)}, f32[2,48,384]{2,1,0:T(8,128)S(1)}, u32[]{:S(2)}, u32[]{:S(2)}) collective-permute-start(f32[2,48,384]{2,1,0:T(8,128)S(1)} %add_add_fusion), channel_id=1, source_target_pairs={{0,3},{1,0},{2,1},{3,2},{4,7},{5,4},{6,5},{7,6},{8,11},{9,8},{10,9... | collective-permute-start | bytes 442376 | tf_op jit(solution)/shard_map/ppermute | solution.py:29
  87.6 13.9 %collective-permute-start.24 = (f32[3,2,48,384]{3,2,1,0:T(8,128)S(1)}, f32[3,2,48,384]{3,2,1,0:T(8,128)S(1)}, u32[]{:S(2)}, u32[]{:S(2)}) collective-permute-start(f32[3,2,48,384]{3,2,1,0:T(8,128)S(1)} %slice.61.refs_0_), channel_id=1, source_target_pairs={{0,32},{16,48},{32,64},{48,80},{64,96},{80,112},{96,0},{112,16},{1... | collective-permute-start | bytes 1327112 | tf_op jit(solution)/shard_map/ppermute | solution.py:21
  87.7 14.9 %collective-permute-start.25 = (f32[3,2,48,384]{3,2,1,0:T(8,128)S(1)}, f32[3,2,48,384]{3,2,1,0:T(8,128)S(1)}, u32[]{:S(2)}, u32[]{:S(2)}) collective-permute-start(f32[3,2,48,384]{3,2,1,0:T(8,128)S(1)} %slice.61.refs_0_), channel_id=1, source_target_pairs={{0,64},{16,80},{32,96},{48,112},{64,0},{80,16},{96,32},{112,48},{1... | collective-permute-start | bytes 1327112 | tf_op jit(solution)/shard_map/ppermute | solution.py:21
  88.7 21.4 %collective-permute-start.26 = (f32[3,2,48,384]{3,2,1,0:T(8,128)S(1)}, f32[3,2,48,384]{3,2,1,0:T(8,128)S(1)}, u32[]{:S(2)}, u32[]{:S(2)}) collective-permute-start(f32[3,2,48,384]{3,2,1,0:T(8,128)S(1)} %slice.61.refs_0_), channel_id=1, source_target_pairs={{0,96},{16,112},{32,0},{48,16},{64,32},{80,48},{96,64},{112,80},{1... | collective-permute-start | bytes 1327112 | tf_op jit(solution)/shard_map/ppermute | solution.py:21
  89.2 21.9 %collective-permute-start.31 = (f32[3,48,384]{2,1,0:T(8,128)S(1)}, f32[3,48,384]{2,1,0:T(8,128)}, u32[]{:S(2)}, u32[]{:S(2)}) collective-permute-start(f32[3,48,384]{2,1,0:T(8,128)S(1)} %bitcast.62), channel_id=1, source_target_pairs={{0,16},{16,0},{32,48},{48,32},{64,80},{80,64},{96,112},{112,96},{1... | collective-permute-start | bytes 663560 | tf_op jit(solution)/shard_map/ppermute | solution.py:25
  94.6 16.9 %collective-permute-start.32 = (f32[3,48,384]{2,1,0:T(8,128)S(1)}, f32[3,48,384]{2,1,0:T(8,128)}, u32[]{:S(2)}, u32[]{:S(2)}) collective-permute-start(f32[3,48,384]{2,1,0:T(8,128)S(1)} %collective-permute-done.21.refs_9_), channel_id=1, source_target_pairs={{0,16},{16,0},{32,48},{48,32},{64,80},{80,64},{96,112},{112,96},{1... | collective-permute-start | bytes 663560 | tf_op jit(solution)/shard_map/ppermute | solution.py:25
  101.5 10.0 %collective-permute-start.33 = (f32[3,48,384]{2,1,0:T(8,128)}, f32[3,48,384]{2,1,0:T(8,128)S(1)}, u32[]{:S(2)}, u32[]{:S(2)}) collective-permute-start(f32[3,48,384]{2,1,0:T(8,128)} %collective-permute-done.22.refs_10_), channel_id=1, source_target_pairs={{0,16},{16,0},{32,48},{48,32},{64,80},{80,64},{96,112},{112,96},{1... | collective-permute-start | bytes 663560 | tf_op jit(solution)/shard_map/ppermute | solution.py:25
  (39 other events, 260.0 us)
Sparse Core Ops, SparseCore 0:
  9.0 35.9 all-gather.6
  60.1 55.8 all-gather.4

commit v2 on v1

--- a/solution.py
+++ b/solution.py
@@ -187,51 +187,44 @@
     pieces, nears = refs[:PROWS], refs[PROWS : 2 * PROWS]
     triangles = refs[2 * PROWS : 2 * PROWS + 4]
     basis_ref, head_ref, corner, own, tri, sems = refs[2 * PROWS + 4 :]
-    copies = []
-    for i in range(4):
-        copies.append(pltpu.make_async_copy(triangles[i], tri.at[i], sems.at[2 * PROWS + i]))
-    for i in range(PROWS):
-        spot = pl.ds(pl.multiple_of(facts_ref[3 + i] * SUB, 16), SUB)
-        copies.append(pltpu.make_async_copy(pieces[i], corner.at[:, :, spot, :], sems.at[2 * i]))
-        copies.append(pltpu.make_async_copy(nears[i], own.at[:, spot, :], sems.at[2 * i + 1]))
+    pairs = [(triangles[i], tri.at[i]) for i in range(4)]
+    for source, kept in ((nears, own), (pieces, corner)):
+        for i in range(PROWS):
+            spot = pl.ds(pl.multiple_of(facts_ref[3 + i] * SUB, 16), SUB)
+            pairs.append((source[i], kept.at[:, spot, :] if kept is own else kept.at[:, :, spot, :]))
+    copies = [pltpu.make_async_copy(*pair, sems.at[i]) for i, pair in enumerate(pairs)]
     for copy in copies:
         copy.start()
+    for copy in copies[: 4 + PROWS]:
+        copy.wait()
+    low = [(tri[0, s], tri[1, s]) for s in range(STEPS)]
+    up = [(tri[2, s], tri[3, s]) for s in range(STEPS)]
+    z0 = own[0]
+    low0 = lhs3(low[0])
+    u0 = dot(low0, rhs3(z0))
+    u0_3 = rhs3(u0)
+    for copy in copies[4 + PROWS :]:
+        copy.wait()
     p, q = facts_ref[0], facts_ref[11]
     row = lax.broadcasted_iota(jnp.int32, (W, W), 0)
     col = lax.broadcasted_iota(jnp.int32, (W, W), 1)
     eye = (row == col).astype(F32)
-    for copy in copies:
-        copy.wait()
-    low = [(tri[0, s], tri[1, s]) for s in range(STEPS)]
-    up = [(tri[2, s], tri[3, s]) for s in range(STEPS)]
-    z0 = own[0]
-    wide = jnp.concatenate([corner[1, 1], corner[2, 0], z0], axis=1)
-    wide = dot(lhs3(low[0]), rhs3(wide))
-    wide3 = rhs3(wide)
-    u01, u02, u0 = wide[:, :W], wide[:, W : 2 * W], wide[:, 2 * W :]
-    tall = jnp.concatenate([corner[0, 0], corner[0, 1]], axis=0)
-    tall = dot(lhs3(tall), rhs3(up[0]))
+    wide = dot(low0, rhs3(jnp.concatenate([corner[1, 1], corner[2, 0]], axis=1)))
+    u01, u02 = wide[:, :W], wide[:, W:]
+    wide3 = jnp.concatenate([rhs3(u02), u0_3], axis=1)
+    tall = dot(lhs3(jnp.concatenate([corner[0, 0], corner[0, 1]], axis=0)), rhs3(up[0]))
     l10, l20 = tall[:W], tall[W:]
-    both = jnp.concatenate([corner[2, 1], own[1]], axis=1) - dot(lhs3(l10), wide3[:, W:])
+    both = jnp.concatenate([corner[2, 1], own[1]], axis=1) - dot(lhs3(l10), wide3)
     x1 = both[:, W:]
     both = dot(lhs3(low[1]), rhs3(both))
     u12, u1 = both[:, :W], both[:, W:]
     l20_3 = lhs3(l20)
-    l21 = dot(lhs3(corner[1, 0] - dot(l20_3, wide3[:, :W])), rhs3(up[1]))
-    x2 = own[2] - dot(l20_3, wide3[:, 2 * W :]) - dot(lhs3(l21), rhs3(u1))
+    l21 = dot(lhs3(corner[1, 0] - dot(l20_3, rhs3(u01))), rhs3(up[1]))
+    x2 = own[2] - dot(l20_3, u0_3) - dot(lhs3(l21), rhs3(u1))
     u2 = dot(lhs3(low[2]), rhs3(x2))
-
-    @pl.when(p == 0)
-    def _():
-        head_ref[...] = jnp.where(q == 0, z0, u0)
-
-    @pl.when(p == 1)
-    def _():
-        head_ref[...] = jnp.where(q == 0, l10, jnp.where(q == 1, x1, u1))
-
-    @pl.when(p >= 2)
-    def _():
-        head_ref[...] = jnp.where(q == 0, l20, jnp.where(q == 1, l21, jnp.where(q == 2, x2, u2)))
+    head = jnp.where(q == 0, l20, jnp.where(q == 1, l21, jnp.where(q == 2, x2, u2)))
+    head = jnp.where(p == 1, jnp.where(q == 0, l10, jnp.where(q == 1, x1, u1)), head)
+    head_ref[...] = jnp.where(p == 0, jnp.where(q == 0, z0, u0), head)
 
     def basis(t, value):
         return jnp.where(q >= STEPS, value, jnp.where(q == t, -eye, 0.0))

time: 147 us -> 147 us (level)
  no operation moved by 1% of the time
where the time goes in v2:
time: 147 us; the launch traced here: 146 us
  starting transfers between devices  49.5 us (34%)
  Pallas kernels  38.8 us (26%)
  waiting for transfers between devices  33.5 us (23%)
  between operations  14.1 us (10%)
  local copies, waits for them, and re-layouts  7.31 us (5%)
  other arithmetic  3.04 us (2%)
    ppermute x6, starting transfers between devices, from_z0(): return lax.ppermute(v, 'pcol', [(y, k * NY + y) for y in range(STEPS)])  15.3 us
    pallas_call x1, Pallas kernels, on_device(): pl.pallas_call(factor_kernel, out_shape=(shape(TOP, W), shape(W, W)), in_...  15.1 us
    ppermute x11, starting transfers between devices, sibling(): return lax.ppermute(v, 'prow', [(p, p ^ 1) for p in range(PROWS)])  13.9 us
    ppermute x12, waiting for transfers between devices, x_shift(): lax.ppermute(v, 'prow', [(p, (p + 2 * k) % PROWS) for p in range(PROWS)])  13.4 us
    ppermute x12, starting transfers between devices, x_shift(): lax.ppermute(v, 'prow', [(p, (p + 2 * k) % PROWS) for p in range(PROWS)])  12.6 us
    ppermute x6, waiting for transfers between devices, y_shift(): lax.ppermute(v, 'pcol', [(z * NY + y, z * NY + (y + k) % NY) for z in ran...  8.92 us
    ppermute x6, waiting for transfers between devices, from_z0(): return lax.ppermute(v, 'pcol', [(y, k * NY + y) for y in range(STEPS)])  8.61 us
    pallas_call x1, Pallas kernels, on_device(): pl.pallas_call(final_kernel, out_shape=shape(ROWS, W), in_specs=[SMEM, HB...  7.98 us
  transfers between devices with their start and end apart: 37, of which 10 were waited for; matrix products, arithmetic and copies ran while one was open for 3% of the time, Pallas kernels for 21%

profile of v2, /device:TPU:11, one launch (start us, length us, event | category | flops | bytes accessed | tf_op | source)
XLA Modules:
  0.0 146.3 jit_solution(12218898919915638885)
XLA Ops:
  6.5 2.0 %slice.51 = f32[1,1,384,384]{3,2,1,0:T(8,128)} slice(f32[1,1,768,384]{3,2,1,0:T(8,128)} %param.4), slice={[0:1], [0:1], [0:384], [0:384]} | slice | bytes 1179648 | tf_op jit(solution)/shard_map/slice | solution.py:306
  9.0 3.6 %collective-permute-start = (f32[96,768]{0,1:T(8,128)S(1)}, f32[96,768]{0,1:T(8,128)S(1)}, u32[]{:S(2)}, u32[]{:S(2)}) collective-permute-start(f32[96,768]{0,1:T(8,128)S(1)} %get-tuple-element.101), channel_id=1, source_target_pairs={{0,4},{1,5},{2,6},{16,20},{17,21},{18,22},{32,36},{33,37},{34,38},... | collective-permute-start | bytes 884744 | tf_op jit(solution)/shard_map/ppermute | solution.py:35
  12.6 2.6 %collective-permute-start.1 = (f32[96,768]{0,1:T(8,128)S(1)}, f32[96,768]{0,1:T(8,128)S(1)}, u32[]{:S(2)}, u32[]{:S(2)}) collective-permute-start(f32[96,768]{0,1:T(8,128)S(1)} %get-tuple-element.100), channel_id=1, source_target_pairs={{0,8},{1,9},{2,10},{16,24},{17,25},{18,26},{32,40},{33,41},{34,42}... | collective-permute-start | bytes 884744 | tf_op jit(solution)/shard_map/ppermute | solution.py:35
  16.8 4.5 %shard_map.46 = (f32[576,384]{1,0:T(8,128)S(1)}, f32[576,384]{1,0:T(8,128)}) custom-call(s32[12]{0:T(128)S(1)} %stack.51.facts_ref, s32[3,384]{1,0:T(4,128)S(1)} %copy-done.5, f32[768,384]{1,0:T(8,128)S(1)} %bitcast.50), custom_call_target="tpu_custom_call" | custom-call | flops 2038431744 | bytes 3145728 | tf_op jit(solution)/shard_map/pallas_call | solution.py:308
  22.2 6.5 %collective-permute-done.1 = f32[96,768]{0,1:T(8,128)S(1)} collective-permute-done((f32[96,768]{0,1:T(8,128)S(1)}, f32[96,768]{0,1:T(8,128)S(1)}, u32[]{:S(2)}, u32[]{:S(2)}) %collective-permute-start.1) | collective-permute-done | bytes 294944 | tf_op jit(solution)/shard_map/ppermute | solution.py:35
  40.8 1.9 %collective-permute-start.9 = (f32[72,384]{1,0:T(8,128)S(1)}, f32[72,384]{1,0:T(8,128)S(1)}, u32[]{:S(2)}, u32[]{:S(2)}) collective-permute-start(f32[72,384]{1,0:T(8,128)S(1)} %slice.57), channel_id=1, source_target_pairs={{0,96},{16,112},{32,0},{48,16},{64,32},{80,48},{96,64},{112,80},{1... | collective-permute-start | bytes 331784 | tf_op jit(solution)/shard_map/ppermute | solution.py:21
  44.1 2.7 %collective-permute-start.11 = (f32[144,384]{1,0:T(8,128)S(1)}, f32[144,384]{1,0:T(8,128)S(1)}, u32[]{:S(2)}, u32[]{:S(2)}) collective-permute-start(f32[144,384]{1,0:T(8,128)S(1)} %get-tuple-element.103), channel_id=1, source_target_pairs={{0,64},{16,80},{32,96},{48,112},{64,0},{80,16},{96,32},{112,48},{1... | collective-permute-start | bytes 663560 | tf_op jit(solution)/shard_map/ppermute | solution.py:21
  46.9 3.9 %collective-permute-start.13 = (f32[72,384]{1,0:T(8,128)S(1)}, f32[72,384]{1,0:T(8,128)S(1)}, u32[]{:S(2)}, u32[]{:S(2)}) collective-permute-start(f32[72,384]{1,0:T(8,128)S(1)} %get-tuple-element.106.a_ref), channel_id=1, source_target_pairs={{0,16},{16,0},{32,48},{48,32},{64,80},{80,64},{96,112},{112,96},{1... | collective-permute-start | bytes 331784 | tf_op jit(solution)/shard_map/ppermute | solution.py:25
  51.6 5.3 %collective-permute-done.12 = f32[144,384]{1,0:T(8,128)S(1)} collective-permute-done((f32[144,384]{1,0:T(8,128)S(1)}, f32[144,384]{1,0:T(8,128)S(1)}, u32[]{:S(2)}, u32[]{:S(2)}) %collective-permute-start.12) | collective-permute-done | bytes 221216 | tf_op jit(solution)/shard_map/ppermute | solution.py:21
  57.0 3.0 %shard_map.48 = f32[72,768]{1,0:T(8,128)} custom-call(s32[12]{0:T(128)S(1)} %stack.51.facts_ref, s32[384,3]{1,0:T(8,128)S(1)} %bitcast.55, f32[72,768]{1,0:T(8,128)S(1)} %bitcast.54, f32[72,384]{1,0:T(8,128)S(1)} %get-tuple-element.106.a_ref, f32[72,384]{1,0:T(8,128)S(1)} %collective-permute-done.13.other_ref, f32[72,384]{1,0:T(8,128)S(1)} %get-tuple-element.105.b_ref, ...), custom_call_target="tpu_custom_call" | custom-call | flops 382205952 | bytes 1048576 | tf_op jit(solution)/shard_map/pallas_call | solution.py:351
  60.1 2.9 %collective-permute-start.15 = (f32[2,48,384]{2,1,0:T(8,128)S(1)}, f32[2,48,384]{2,1,0:T(8,128)S(1)}, u32[]{:S(2)}, u32[]{:S(2)}) collective-permute-start(f32[2,48,384]{2,1,0:T(8,128)S(1)} %fusion.5), channel_id=1, source_target_pairs={{0,4},{1,5},{2,6},{16,20},{17,21},{18,22},{32,36},{33,37},{34,38},... | collective-permute-start | bytes 442376 | tf_op jit(solution)/shard_map/ppermute | solution.py:35
  63.0 3.5 %collective-permute-start.16 = (f32[2,48,384]{2,1,0:T(8,128)S(1)}, f32[2,48,384]{2,1,0:T(8,128)S(1)}, u32[]{:S(2)}, u32[]{:S(2)}) collective-permute-start(f32[2,48,384]{2,1,0:T(8,128)S(1)} %fusion.5), channel_id=1, source_target_pairs={{0,8},{1,9},{2,10},{16,24},{17,25},{18,26},{32,40},{33,41},{34,42}... | collective-permute-start | bytes 442376 | tf_op jit(solution)/shard_map/ppermute | solution.py:35
  70.0 1.8 %collective-permute-start.18 = (f32[2,48,384]{2,1,0:T(8,128)S(1)}, f32[2,48,384]{2,1,0:T(8,128)S(1)}, u32[]{:S(2)}, u32[]{:S(2)}) collective-permute-start(f32[2,48,384]{2,1,0:T(8,128)S(1)} %add_add_fusion), channel_id=1, source_target_pairs={{0,1},{1,2},{2,3},{3,0},{4,5},{5,6},{6,7},{7,4},{8,9},{9,10},{10,1... | collective-permute-start | bytes 442376 | tf_op jit(solution)/shard_map/ppermute | solution.py:29
  71.8 2.0 %collective-permute-start.22 = (f32[3,48,384]{2,1,0:T(8,128)S(1)}, f32[3,48,384]{2,1,0:T(8,128)}, u32[]{:S(2)}, u32[]{:S(2)}) collective-permute-start(f32[3,48,384]{2,1,0:T(8,128)S(1)} %bitcast.60), channel_id=1, source_target_pairs={{0,64},{16,80},{32,96},{48,112},{64,0},{80,16},{96,32},{112,48},{1... | collective-permute-start | bytes 663560 | tf_op jit(solution)/shard_map/ppermute | solution.py:21
  73.9 2.1 %collective-permute-start.23 = (f32[3,48,384]{2,1,0:T(8,128)S(1)}, f32[3,48,384]{2,1,0:T(8,128)}, u32[]{:S(2)}, u32[]{:S(2)}) collective-permute-start(f32[3,48,384]{2,1,0:T(8,128)S(1)} %bitcast.61), channel_id=1, source_target_pairs={{0,96},{16,112},{32,0},{48,16},{64,32},{80,48},{96,64},{112,80},{1... | collective-permute-start | bytes 663560 | tf_op jit(solution)/shard_map/ppermute | solution.py:21
  75.9 2.6 %collective-permute-start.19 = (f32[2,48,384]{2,1,0:T(8,128)S(1)}, f32[2,48,384]{2,1,0:T(8,128)S(1)}, u32[]{:S(2)}, u32[]{:S(2)}) collective-permute-start(f32[2,48,384]{2,1,0:T(8,128)S(1)} %add_add_fusion), channel_id=1, source_target_pairs={{0,2},{1,3},{2,0},{3,1},{4,6},{5,7},{6,4},{7,5},{8,10},{9,11},{10,... | collective-permute-start | bytes 442376 | tf_op jit(solution)/shard_map/ppermute | solution.py:29
  78.5 3.6 %collective-permute-done.19 = f32[2,48,384]{2,1,0:T(8,128)S(1)} collective-permute-done((f32[2,48,384]{2,1,0:T(8,128)S(1)}, f32[2,48,384]{2,1,0:T(8,128)S(1)}, u32[]{:S(2)}, u32[]{:S(2)}) %collective-permute-start.19) | collective-permute-done | bytes 147488 | tf_op jit(solution)/shard_map/ppermute | solution.py:29
  82.1 5.3 %collective-permute-done.20 = f32[2,48,384]{2,1,0:T(8,128)S(1)} collective-permute-done((f32[2,48,384]{2,1,0:T(8,128)S(1)}, f32[2,48,384]{2,1,0:T(8,128)S(1)}, u32[]{:S(2)}, u32[]{:S(2)}) %collective-permute-start.20) | collective-permute-done | bytes 147488 | tf_op jit(solution)/shard_map/ppermute | solution.py:29
  89.2 5.4 %collective-permute-start.31 = (f32[3,48,384]{2,1,0:T(8,128)S(1)}, f32[3,48,384]{2,1,0:T(8,128)}, u32[]{:S(2)}, u32[]{:S(2)}) collective-permute-start(f32[3,48,384]{2,1,0:T(8,128)S(1)} %bitcast.62), channel_id=1, source_target_pairs={{0,16},{16,0},{32,48},{48,32},{64,80},{80,64},{96,112},{112,96},{1... | collective-permute-start | bytes 663560 | tf_op jit(solution)/shard_map/ppermute | solution.py:25
  94.6 6.9 %shard_map.49.here_ref = f32[768,384]{1,0:T(8,128)} custom-call(s32[12]{0:T(128)} %copy-done.6, s32[3,384]{1,0:T(4,128)} %pivots_ref.3, f32[768,384]{1,0:T(8,128)} %bitcast.48, f32[8,384,384]{2,1,0:T(8,128)} %bitcast.65), custom_call_target="tpu_custom_call" | custom-call | flops 2038431744 | bytes 5242880 | tf_op jit(solution)/shard_map/pallas_call | solution.py:379
  102.6 7.5 %collective-permute-done.26.refs_3_ = f32[3,2,48,384]{3,2,1,0:T(8,128)S(1)} collective-permute-done((f32[3,2,48,384]{3,2,1,0:T(8,128)S(1)}, f32[3,2,48,384]{3,2,1,0:T(8,128)S(1)}, u32[]{:S(2)}, u32[]{:S(2)}) %collective-permute-start.26) | collective-permute-done | bytes 442400 | tf_op jit(solution)/shard_map/ppermute | solution.py:21
  112.0 2.4 %collective-permute-done.34.refs_15_ = f32[3,48,384]{2,1,0:T(8,128)S(1)} collective-permute-done((f32[3,48,384]{2,1,0:T(8,128)}, f32[3,48,384]{2,1,0:T(8,128)S(1)}, u32[]{:S(2)}, u32[]{:S(2)}) %collective-permute-start.34) | collective-permute-done | bytes 221216 | tf_op jit(solution)/shard_map/ppermute | solution.py:25
  116.3 15.1 %shard_map.50 = (f32[1152,384]{1,0:T(8,128)}, f32[384,384]{1,0:T(8,128)}) custom-call(s32[12]{0:T(128)} %copy-done.6, f32[3,2,48,384]{3,2,1,0:T(8,128)} %copy-done.12, f32[3,2,48,384]{3,2,1,0:T(8,128)} %copy-done.16, f32[3,2,48,384]{3,2,1,0:T(8,128)} %copy-done.17, f32[3,2,48,384]{3,2,1,0:T(8,128)} %copy-done.18, f32[3,2,48,384]{3,2,1,0:T(8,128)} %copy-done.19, ...), custom_call_target="tpu_custom_call" | custom-call | flops 6794772480 | bytes 11534336 | tf_op jit(solution)/shard_map/pallas_call | solution.py:391
  131.4 8.0 %shard_map.51 = f32[768,384]{1,0:T(8,128)} custom-call(s32[12]{0:T(128)} %copy-done.6, f32[1152,768]{1,0:T(8,128)} %all-gather.5.cloned.1.call-done.panel_ref, f32[1152,384]{1,0:T(8,128)} %get-tuple-element.96.basis_ref, f32[768,384]{1,0:T(8,128)} %shard_map.49.here_ref, f32[384,384]{1,0:T(8,128)} %get-tuple-element.98.head_ref), custom_call_target="tpu_custom_call" | custom-call | flops 2038431744 | bytes 8388608 | tf_op jit(solution)/shard_map/pallas_call | solution.py:405
  (135 shorter events, 27.1 us)
Async XLA Ops:
  6.5 88.1 %all-gather.7.cloned.1.call-start = ((), (), s32[]{:S(2)}) async-start(), calls=%async_computation.1 | async-start | bytes 5308416 | tf_op jit(solution)/shard_map/all_gather | solution.py:306
  8.6 122.8 %all-gather.5.cloned.1.call-start = ((), (), s32[]{:S(2)}) async-start(), calls=%async_computation | async-start | bytes 3760128 | tf_op jit(solution)/shard_map/all_gather | solution.py:358
  9.0 13.2 %collective-permute-start = (f32[96,768]{0,1:T(8,128)S(1)}, f32[96,768]{0,1:T(8,128)S(1)}, u32[]{:S(2)}, u32[]{:S(2)}) collective-permute-start(f32[96,768]{0,1:T(8,128)S(1)} %get-tuple-element.101), channel_id=1, source_target_pairs={{0,4},{1,5},{2,6},{16,20},{17,21},{18,22},{32,36},{33,37},{34,38},... | collective-permute-start | bytes 884744 | tf_op jit(solution)/shard_map/ppermute | solution.py:35
  12.6 16.2 %collective-permute-start.1 = (f32[96,768]{0,1:T(8,128)S(1)}, f32[96,768]{0,1:T(8,128)S(1)}, u32[]{:S(2)}, u32[]{:S(2)}) collective-permute-start(f32[96,768]{0,1:T(8,128)S(1)} %get-tuple-element.100), channel_id=1, source_target_pairs={{0,8},{1,9},{2,10},{16,24},{17,25},{18,26},{32,40},{33,41},{34,42}... | collective-permute-start | bytes 884744 | tf_op jit(solution)/shard_map/ppermute | solution.py:35
  15.2 13.5 %collective-permute-start.2 = (f32[96,768]{0,1:T(8,128)S(1)}, f32[96,768]{0,1:T(8,128)S(1)}, u32[]{:S(2)}, u32[]{:S(2)}) collective-permute-start(f32[96,768]{0,1:T(8,128)S(1)} %get-tuple-element.99), channel_id=1, source_target_pairs={{0,12},{1,13},{2,14},{16,28},{17,29},{18,30},{32,44},{33,45},{34,4... | collective-permute-start | bytes 884744 | tf_op jit(solution)/shard_map/ppermute | solution.py:35
  28.8 9.5 %collective-permute-start.6 = (f32[576,384]{1,0:T(8,128)}, f32[576,384]{1,0:T(8,128)}, u32[]{:S(2)}, u32[]{:S(2)}) collective-permute-start(f32[576,384]{1,0:T(8,128)} %get-tuple-element.57), channel_id=1, source_target_pairs={{0,16},{16,0},{32,48},{48,32},{64,80},{80,64},{96,112},{112,96},{1... | collective-permute-start | bytes 2654216 | tf_op jit(solution)/shard_map/ppermute | solution.py:25
  38.4 8.4 %collective-permute-start.7 = (f32[72,384]{1,0:T(8,128)S(1)}, f32[72,384]{1,0:T(8,128)S(1)}, u32[]{:S(2)}, u32[]{:S(2)}) collective-permute-start(f32[72,384]{1,0:T(8,128)S(1)} %slice.57), channel_id=1, source_target_pairs={{0,32},{16,48},{32,64},{48,80},{64,96},{80,112},{96,0},{112,16},{1... | collective-permute-start | bytes 331784 | tf_op jit(solution)/shard_map/ppermute | solution.py:21
  39.7 7.1 %collective-permute-start.8 = (f32[72,384]{1,0:T(8,128)S(1)}, f32[72,384]{1,0:T(8,128)S(1)}, u32[]{:S(2)}, u32[]{:S(2)}) collective-permute-start(f32[72,384]{1,0:T(8,128)S(1)} %slice.57), channel_id=1, source_target_pairs={{0,64},{16,80},{32,96},{48,112},{64,0},{80,16},{96,32},{112,48},{1... | collective-permute-start | bytes 331784 | tf_op jit(solution)/shard_map/ppermute | solution.py:21
  44.1 7.0 %collective-permute-start.10 = (f32[144,384]{1,0:T(8,128)S(1)}, f32[144,384]{1,0:T(8,128)S(1)}, u32[]{:S(2)}, u32[]{:S(2)}) collective-permute-start(f32[144,384]{1,0:T(8,128)S(1)} %get-tuple-element.104), channel_id=1, source_target_pairs={{0,32},{16,48},{32,64},{48,80},{64,96},{80,112},{96,0},{112,16},{1... | collective-permute-start | bytes 663560 | tf_op jit(solution)/shard_map/ppermute | solution.py:21
  44.1 7.5 %collective-permute-start.11 = (f32[144,384]{1,0:T(8,128)S(1)}, f32[144,384]{1,0:T(8,128)S(1)}, u32[]{:S(2)}, u32[]{:S(2)}) collective-permute-start(f32[144,384]{1,0:T(8,128)S(1)} %get-tuple-element.103), channel_id=1, source_target_pairs={{0,64},{16,80},{32,96},{48,112},{64,0},{80,16},{96,32},{112,48},{1... | collective-permute-start | bytes 663560 | tf_op jit(solution)/shard_map/ppermute | solution.py:21
  46.8 10.1 %collective-permute-start.12 = (f32[144,384]{1,0:T(8,128)S(1)}, f32[144,384]{1,0:T(8,128)S(1)}, u32[]{:S(2)}, u32[]{:S(2)}) collective-permute-start(f32[144,384]{1,0:T(8,128)S(1)} %get-tuple-element.102), channel_id=1, source_target_pairs={{0,96},{16,112},{32,0},{48,16},{64,32},{80,48},{96,64},{112,80},{1... | collective-permute-start | bytes 663560 | tf_op jit(solution)/shard_map/ppermute | solution.py:21
  46.9 10.0 %collective-permute-start.13 = (f32[72,384]{1,0:T(8,128)S(1)}, f32[72,384]{1,0:T(8,128)S(1)}, u32[]{:S(2)}, u32[]{:S(2)}) collective-permute-start(f32[72,384]{1,0:T(8,128)S(1)} %get-tuple-element.106.a_ref), channel_id=1, source_target_pairs={{0,16},{16,0},{32,48},{48,32},{64,80},{80,64},{96,112},{112,96},{1... | collective-permute-start | bytes 331784 | tf_op jit(solution)/shard_map/ppermute | solution.py:25
  60.1 7.8 %collective-permute-start.15 = (f32[2,48,384]{2,1,0:T(8,128)S(1)}, f32[2,48,384]{2,1,0:T(8,128)S(1)}, u32[]{:S(2)}, u32[]{:S(2)}) collective-permute-start(f32[2,48,384]{2,1,0:T(8,128)S(1)} %fusion.5), channel_id=1, source_target_pairs={{0,4},{1,5},{2,6},{16,20},{17,21},{18,22},{32,36},{33,37},{34,38},... | collective-permute-start | bytes 442376 | tf_op jit(solution)/shard_map/ppermute | solution.py:35
  70.0 8.5 %collective-permute-start.18 = (f32[2,48,384]{2,1,0:T(8,128)S(1)}, f32[2,48,384]{2,1,0:T(8,128)S(1)}, u32[]{:S(2)}, u32[]{:S(2)}) collective-permute-start(f32[2,48,384]{2,1,0:T(8,128)S(1)} %add_add_fusion), channel_id=1, source_target_pairs={{0,1},{1,2},{2,3},{3,0},{4,5},{5,6},{6,7},{7,4},{8,9},{9,10},{10,1... | collective-permute-start | bytes 442376 | tf_op jit(solution)/shard_map/ppermute | solution.py:29
  71.8 15.6 %collective-permute-start.21 = (f32[3,48,384]{2,1,0:T(8,128)S(1)}, f32[3,48,384]{2,1,0:T(8,128)S(1)}, u32[]{:S(2)}, u32[]{:S(2)}) collective-permute-start(f32[3,48,384]{2,1,0:T(8,128)S(1)} %bitcast.59), channel_id=1, source_target_pairs={{0,32},{16,48},{32,64},{48,80},{64,96},{80,112},{96,0},{112,16},{1... | collective-permute-start | bytes 663560 | tf_op jit(solution)/shard_map/ppermute | solution.py:21
  71.8 15.6 %collective-permute-start.22 = (f32[3,48,384]{2,1,0:T(8,128)S(1)}, f32[3,48,384]{2,1,0:T(8,128)}, u32[]{:S(2)}, u32[]{:S(2)}) collective-permute-start(f32[3,48,384]{2,1,0:T(8,128)S(1)} %bitcast.60), channel_id=1, source_target_pairs={{0,64},{16,80},{32,96},{48,112},{64,0},{80,16},{96,32},{112,48},{1... | collective-permute-start | bytes 663560 | tf_op jit(solution)/shard_map/ppermute | solution.py:21
  73.9 13.6 %collective-permute-start.23 = (f32[3,48,384]{2,1,0:T(8,128)S(1)}, f32[3,48,384]{2,1,0:T(8,128)}, u32[]{:S(2)}, u32[]{:S(2)}) collective-permute-start(f32[3,48,384]{2,1,0:T(8,128)S(1)} %bitcast.61), channel_id=1, source_target_pairs={{0,96},{16,112},{32,0},{48,16},{64,32},{80,48},{96,64},{112,80},{1... | collective-permute-start | bytes 663560 | tf_op jit(solution)/shard_map/ppermute | solution.py:21
  78.5 8.9 %collective-permute-start.20 = (f32[2,48,384]{2,1,0:T(8,128)S(1)}, f32[2,48,384]{2,1,0:T(8,128)S(1)}, u32[]{:S(2)}, u32[]{:S(2)}) collective-permute-start(f32[2,48,384]{2,1,0:T(8,128)S(1)} %add_add_fusion), channel_id=1, source_target_pairs={{0,3},{1,0},{2,1},{3,2},{4,7},{5,4},{6,5},{7,6},{8,11},{9,8},{10,9... | collective-permute-start | bytes 442376 | tf_op jit(solution)/shard_map/ppermute | solution.py:29
  87.6 13.9 %collective-permute-start.24 = (f32[3,2,48,384]{3,2,1,0:T(8,128)S(1)}, f32[3,2,48,384]{3,2,1,0:T(8,128)S(1)}, u32[]{:S(2)}, u32[]{:S(2)}) collective-permute-start(f32[3,2,48,384]{3,2,1,0:T(8,128)S(1)} %slice.61.refs_0_), channel_id=1, source_target_pairs={{0,32},{16,48},{32,64},{48,80},{64,96},{80,112},{96,0},{112,16},{1... | collective-permute-start | bytes 1327112 | tf_op jit(solution)/shard_map/ppermute | solution.py:21
  87.7 14.9 %collective-permute-start.25 = (f32[3,2,48,384]{3,2,1,0:T(8,128)S(1)}, f32[3,2,48,384]{3,2,1,0:T(8,128)S(1)}, u32[]{:S(2)}, u32[]{:S(2)}) collective-permute-start(f32[3,2,48,384]{3,2,1,0:T(8,128)S(1)} %slice.61.refs_0_), channel_id=1, source_target_pairs={{0,64},{16,80},{32,96},{48,112},{64,0},{80,16},{96,32},{112,48},{1... | collective-permute-start | bytes 1327112 | tf_op jit(solution)/shard_map/ppermute | solution.py:21
  88.7 21.4 %collective-permute-start.26 = (f32[3,2,48,384]{3,2,1,0:T(8,128)S(1)}, f32[3,2,48,384]{3,2,1,0:T(8,128)S(1)}, u32[]{:S(2)}, u32[]{:S(2)}) collective-permute-start(f32[3,2,48,384]{3,2,1,0:T(8,128)S(1)} %slice.61.refs_0_), channel_id=1, source_target_pairs={{0,96},{16,112},{32,0},{48,16},{64,32},{80,48},{96,64},{112,80},{1... | collective-permute-start | bytes 1327112 | tf_op jit(solution)/shard_map/ppermute | solution.py:21
  89.2 21.9 %collective-permute-start.31 = (f32[3,48,384]{2,1,0:T(8,128)S(1)}, f32[3,48,384]{2,1,0:T(8,128)}, u32[]{:S(2)}, u32[]{:S(2)}) collective-permute-start(f32[3,48,384]{2,1,0:T(8,128)S(1)} %bitcast.62), channel_id=1, source_target_pairs={{0,16},{16,0},{32,48},{48,32},{64,80},{80,64},{96,112},{112,96},{1... | collective-permute-start | bytes 663560 | tf_op jit(solution)/shard_map/ppermute | solution.py:25
  94.6 16.9 %collective-permute-start.32 = (f32[3,48,384]{2,1,0:T(8,128)S(1)}, f32[3,48,384]{2,1,0:T(8,128)}, u32[]{:S(2)}, u32[]{:S(2)}) collective-permute-start(f32[3,48,384]{2,1,0:T(8,128)S(1)} %collective-permute-done.21.refs_9_), channel_id=1, source_target_pairs={{0,16},{16,0},{32,48},{48,32},{64,80},{80,64},{96,112},{112,96},{1... | collective-permute-start | bytes 663560 | tf_op jit(solution)/shard_map/ppermute | solution.py:25
  101.5 10.0 %collective-permute-start.33 = (f32[3,48,384]{2,1,0:T(8,128)}, f32[3,48,384]{2,1,0:T(8,128)S(1)}, u32[]{:S(2)}, u32[]{:S(2)}) collective-permute-start(f32[3,48,384]{2,1,0:T(8,128)} %collective-permute-done.22.refs_10_), channel_id=1, source_target_pairs={{0,16},{16,0},{32,48},{48,32},{64,80},{80,64},{96,112},{112,96},{1... | collective-permute-start | bytes 663560 | tf_op jit(solution)/shard_map/ppermute | solution.py:25
  (39 other events, 260.0 us)
Sparse Core Ops, SparseCore 0:
  9.0 35.9 all-gather.6
  60.1 55.8 all-gather.4

commit v3 on v2

--- a/solution.py
+++ b/solution.py
@@ -245,14 +245,14 @@
     keep(0, g0)
 
 
-def final_kernel(facts_ref, panel_ref, basis_ref, here_ref, head_ref, out_ref, panel, sems):
+def final_kernel(facts_ref, panel_hbm, basis_hbm, here_hbm, head_hbm, out_ref, panel, basis_ref, here_ref, head_ref, sems):
     p, q = facts_ref[0], facts_ref[11]
-    copies = [
-        pltpu.make_async_copy(panel_ref.at[:, i * W : (i + 1) * W], panel.at[i], sems.at[i])
-        for i in range(2)
-    ]
+    pairs = [(panel_hbm.at[:, i * W : (i + 1) * W], panel.at[i]) for i in range(2)]
+    pairs = [(basis_hbm, basis_ref), pairs[0], pairs[1], (here_hbm, here_ref), (head_hbm, head_ref)]
+    copies = [pltpu.make_async_copy(*pair, sems.at[i]) for i, pair in enumerate(pairs)]
     for copy in copies:
         copy.start()
+    copies[0].wait()
     g = halves(basis_ref[...])
 
     def rows(i):
@@ -260,7 +260,8 @@
         a = halves(panel[i].T)
         out_ref[span, :] = jnp.where(q >= STEPS, here_ref[span, :], 0.0) - mm3(a, g)
 
-    copies[0].wait()
+    for copy in (copies[1], copies[3], copies[4]):
+        copy.wait()
 
     @pl.when(p < STEPS)
     def _():
@@ -270,7 +271,7 @@
     def _():
         rows(0)
 
-    copies[1].wait()
+    copies[2].wait()
     rows(1)
 
 
@@ -405,8 +406,14 @@
     result = pl.pallas_call(
         final_kernel,
         out_shape=shape(ROWS, W),
-        in_specs=[SMEM, HBM] + [WHOLE] * 3,
-        scratch_shapes=[pltpu.VMEM((2, TOP, W), F32), pltpu.SemaphoreType.DMA((2,))],
+        in_specs=[SMEM] + [HBM] * 4,
+        scratch_shapes=[
+            pltpu.VMEM((2, TOP, W), F32),
+            pltpu.VMEM((TOP, W), F32),
+            pltpu.VMEM((ROWS, W), F32),
+            pltpu.VMEM((W, W), F32),
+            pltpu.SemaphoreType.DMA((5,)),
+        ],
         compiler_params=params(60),
         cost_estimate=cost(6 * ROWS * TOP * W, 8 << 20),
     )(facts, panel, basis, here, head)

time: 147 us -> 147 us (level)
  no operation moved by 1% of the time
where the time goes in v3:
time: 147 us; the launch traced here: 146 us
  starting transfers between devices  49.5 us (34%)
  Pallas kernels  39.1 us (27%)
  waiting for transfers between devices  33.5 us (23%)
  between operations  14.1 us (10%)
  local copies, waits for them, and re-layouts  7.31 us (5%)
  other arithmetic  3.04 us (2%)
    ppermute x6, starting transfers between devices, from_z0(): return lax.ppermute(v, 'pcol', [(y, k * NY + y) for y in range(STEPS)])  15.3 us
    pallas_call x1, Pallas kernels, on_device(): pl.pallas_call(factor_kernel, out_shape=(shape(TOP, W), shape(W, W)), in_...  15.1 us
    ppermute x11, starting transfers between devices, sibling(): return lax.ppermute(v, 'prow', [(p, p ^ 1) for p in range(PROWS)])  13.9 us
    ppermute x12, waiting for transfers between devices, x_shift(): lax.ppermute(v, 'prow', [(p, (p + 2 * k) % PROWS) for p in range(PROWS)])  13.4 us
    ppermute x12, starting transfers between devices, x_shift(): lax.ppermute(v, 'prow', [(p, (p + 2 * k) % PROWS) for p in range(PROWS)])  12.6 us
    ppermute x6, waiting for transfers between devices, y_shift(): lax.ppermute(v, 'pcol', [(z * NY + y, z * NY + (y + k) % NY) for z in ran...  8.92 us
    ppermute x6, waiting for transfers between devices, from_z0(): return lax.ppermute(v, 'pcol', [(y, k * NY + y) for y in range(STEPS)])  8.61 us
    pallas_call x1, Pallas kernels, on_device(): pl.pallas_call(final_kernel, out_shape=shape(ROWS, W), in_specs=[SMEM] +...  8.22 us
  transfers between devices with their start and end apart: 37, of which 10 were waited for; matrix products, arithmetic and copies ran while one was open for 3% of the time, Pallas kernels for 21%

profile of v3, /device:TPU:11, one launch (start us, length us, event | category | flops | bytes accessed | tf_op | source)
XLA Modules:
  0.0 146.5 jit_solution(4342865424463470401)
XLA Ops:
  6.5 2.0 %slice.51 = f32[1,1,384,384]{3,2,1,0:T(8,128)} slice(f32[1,1,768,384]{3,2,1,0:T(8,128)} %param.4), slice={[0:1], [0:1], [0:384], [0:384]} | slice | bytes 1179648 | tf_op jit(solution)/shard_map/slice | solution.py:307
  9.0 3.6 %collective-permute-start = (f32[96,768]{0,1:T(8,128)S(1)}, f32[96,768]{0,1:T(8,128)S(1)}, u32[]{:S(2)}, u32[]{:S(2)}) collective-permute-start(f32[96,768]{0,1:T(8,128)S(1)} %get-tuple-element.101), channel_id=1, source_target_pairs={{0,4},{1,5},{2,6},{16,20},{17,21},{18,22},{32,36},{33,37},{34,38},... | collective-permute-start | bytes 884744 | tf_op jit(solution)/shard_map/ppermute | solution.py:35
  12.6 2.6 %collective-permute-start.1 = (f32[96,768]{0,1:T(8,128)S(1)}, f32[96,768]{0,1:T(8,128)S(1)}, u32[]{:S(2)}, u32[]{:S(2)}) collective-permute-start(f32[96,768]{0,1:T(8,128)S(1)} %get-tuple-element.100), channel_id=1, source_target_pairs={{0,8},{1,9},{2,10},{16,24},{17,25},{18,26},{32,40},{33,41},{34,42}... | collective-permute-start | bytes 884744 | tf_op jit(solution)/shard_map/ppermute | solution.py:35
  16.8 4.5 %shard_map.46 = (f32[576,384]{1,0:T(8,128)S(1)}, f32[576,384]{1,0:T(8,128)}) custom-call(s32[12]{0:T(128)S(1)} %stack.51.facts_ref, s32[3,384]{1,0:T(4,128)S(1)} %copy-done.5, f32[768,384]{1,0:T(8,128)S(1)} %bitcast.50), custom_call_target="tpu_custom_call" | custom-call | flops 2038431744 | bytes 3145728 | tf_op jit(solution)/shard_map/pallas_call | solution.py:309
  22.2 6.5 %collective-permute-done.1 = f32[96,768]{0,1:T(8,128)S(1)} collective-permute-done((f32[96,768]{0,1:T(8,128)S(1)}, f32[96,768]{0,1:T(8,128)S(1)}, u32[]{:S(2)}, u32[]{:S(2)}) %collective-permute-start.1) | collective-permute-done | bytes 294944 | tf_op jit(solution)/shard_map/ppermute | solution.py:35
  40.8 1.9 %collective-permute-start.9 = (f32[72,384]{1,0:T(8,128)S(1)}, f32[72,384]{1,0:T(8,128)S(1)}, u32[]{:S(2)}, u32[]{:S(2)}) collective-permute-start(f32[72,384]{1,0:T(8,128)S(1)} %slice.57), channel_id=1, source_target_pairs={{0,96},{16,112},{32,0},{48,16},{64,32},{80,48},{96,64},{112,80},{1... | collective-permute-start | bytes 331784 | tf_op jit(solution)/shard_map/ppermute | solution.py:21
  44.1 2.7 %collective-permute-start.11 = (f32[144,384]{1,0:T(8,128)S(1)}, f32[144,384]{1,0:T(8,128)S(1)}, u32[]{:S(2)}, u32[]{:S(2)}) collective-permute-start(f32[144,384]{1,0:T(8,128)S(1)} %get-tuple-element.103), channel_id=1, source_target_pairs={{0,64},{16,80},{32,96},{48,112},{64,0},{80,16},{96,32},{112,48},{1... | collective-permute-start | bytes 663560 | tf_op jit(solution)/shard_map/ppermute | solution.py:21
  46.9 3.9 %collective-permute-start.13 = (f32[72,384]{1,0:T(8,128)S(1)}, f32[72,384]{1,0:T(8,128)S(1)}, u32[]{:S(2)}, u32[]{:S(2)}) collective-permute-start(f32[72,384]{1,0:T(8,128)S(1)} %get-tuple-element.106.a_ref), channel_id=1, source_target_pairs={{0,16},{16,0},{32,48},{48,32},{64,80},{80,64},{96,112},{112,96},{1... | collective-permute-start | bytes 331784 | tf_op jit(solution)/shard_map/ppermute | solution.py:25
  51.6 5.3 %collective-permute-done.12 = f32[144,384]{1,0:T(8,128)S(1)} collective-permute-done((f32[144,384]{1,0:T(8,128)S(1)}, f32[144,384]{1,0:T(8,128)S(1)}, u32[]{:S(2)}, u32[]{:S(2)}) %collective-permute-start.12) | collective-permute-done | bytes 221216 | tf_op jit(solution)/shard_map/ppermute | solution.py:21
  57.0 3.0 %shard_map.48 = f32[72,768]{1,0:T(8,128)} custom-call(s32[12]{0:T(128)S(1)} %stack.51.facts_ref, s32[384,3]{1,0:T(8,128)S(1)} %bitcast.55, f32[72,768]{1,0:T(8,128)S(1)} %bitcast.54, f32[72,384]{1,0:T(8,128)S(1)} %get-tuple-element.106.a_ref, f32[72,384]{1,0:T(8,128)S(1)} %collective-permute-done.13.other_ref, f32[72,384]{1,0:T(8,128)S(1)} %get-tuple-element.105.b_ref, ...), custom_call_target="tpu_custom_call" | custom-call | flops 382205952 | bytes 1048576 | tf_op jit(solution)/shard_map/pallas_call | solution.py:352
  60.1 2.9 %collective-permute-start.15 = (f32[2,48,384]{2,1,0:T(8,128)S(1)}, f32[2,48,384]{2,1,0:T(8,128)S(1)}, u32[]{:S(2)}, u32[]{:S(2)}) collective-permute-start(f32[2,48,384]{2,1,0:T(8,128)S(1)} %fusion.5), channel_id=1, source_target_pairs={{0,4},{1,5},{2,6},{16,20},{17,21},{18,22},{32,36},{33,37},{34,38},... | collective-permute-start | bytes 442376 | tf_op jit(solution)/shard_map/ppermute | solution.py:35
  63.0 3.5 %collective-permute-start.16 = (f32[2,48,384]{2,1,0:T(8,128)S(1)}, f32[2,48,384]{2,1,0:T(8,128)S(1)}, u32[]{:S(2)}, u32[]{:S(2)}) collective-permute-start(f32[2,48,384]{2,1,0:T(8,128)S(1)} %fusion.5), channel_id=1, source_target_pairs={{0,8},{1,9},{2,10},{16,24},{17,25},{18,26},{32,40},{33,41},{34,42}... | collective-permute-start | bytes 442376 | tf_op jit(solution)/shard_map/ppermute | solution.py:35
  70.0 1.8 %collective-permute-start.18 = (f32[2,48,384]{2,1,0:T(8,128)S(1)}, f32[2,48,384]{2,1,0:T(8,128)S(1)}, u32[]{:S(2)}, u32[]{:S(2)}) collective-permute-start(f32[2,48,384]{2,1,0:T(8,128)S(1)} %add_add_fusion), channel_id=1, source_target_pairs={{0,1},{1,2},{2,3},{3,0},{4,5},{5,6},{6,7},{7,4},{8,9},{9,10},{10,1... | collective-permute-start | bytes 442376 | tf_op jit(solution)/shard_map/ppermute | solution.py:29
  71.8 2.0 %collective-permute-start.22 = (f32[3,48,384]{2,1,0:T(8,128)S(1)}, f32[3,48,384]{2,1,0:T(8,128)}, u32[]{:S(2)}, u32[]{:S(2)}) collective-permute-start(f32[3,48,384]{2,1,0:T(8,128)S(1)} %bitcast.60), channel_id=1, source_target_pairs={{0,64},{16,80},{32,96},{48,112},{64,0},{80,16},{96,32},{112,48},{1... | collective-permute-start | bytes 663560 | tf_op jit(solution)/shard_map/ppermute | solution.py:21
  73.9 2.1 %collective-permute-start.23 = (f32[3,48,384]{2,1,0:T(8,128)S(1)}, f32[3,48,384]{2,1,0:T(8,128)}, u32[]{:S(2)}, u32[]{:S(2)}) collective-permute-start(f32[3,48,384]{2,1,0:T(8,128)S(1)} %bitcast.61), channel_id=1, source_target_pairs={{0,96},{16,112},{32,0},{48,16},{64,32},{80,48},{96,64},{112,80},{1... | collective-permute-start | bytes 663560 | tf_op jit(solution)/shard_map/ppermute | solution.py:21
  75.9 2.6 %collective-permute-start.19 = (f32[2,48,384]{2,1,0:T(8,128)S(1)}, f32[2,48,384]{2,1,0:T(8,128)S(1)}, u32[]{:S(2)}, u32[]{:S(2)}) collective-permute-start(f32[2,48,384]{2,1,0:T(8,128)S(1)} %add_add_fusion), channel_id=1, source_target_pairs={{0,2},{1,3},{2,0},{3,1},{4,6},{5,7},{6,4},{7,5},{8,10},{9,11},{10,... | collective-permute-start | bytes 442376 | tf_op jit(solution)/shard_map/ppermute | solution.py:29
  78.5 3.6 %collective-permute-done.19 = f32[2,48,384]{2,1,0:T(8,128)S(1)} collective-permute-done((f32[2,48,384]{2,1,0:T(8,128)S(1)}, f32[2,48,384]{2,1,0:T(8,128)S(1)}, u32[]{:S(2)}, u32[]{:S(2)}) %collective-permute-start.19) | collective-permute-done | bytes 147488 | tf_op jit(solution)/shard_map/ppermute | solution.py:29
  82.1 5.3 %collective-permute-done.20 = f32[2,48,384]{2,1,0:T(8,128)S(1)} collective-permute-done((f32[2,48,384]{2,1,0:T(8,128)S(1)}, f32[2,48,384]{2,1,0:T(8,128)S(1)}, u32[]{:S(2)}, u32[]{:S(2)}) %collective-permute-start.20) | collective-permute-done | bytes 147488 | tf_op jit(solution)/shard_map/ppermute | solution.py:29
  89.2 5.4 %collective-permute-start.31 = (f32[3,48,384]{2,1,0:T(8,128)S(1)}, f32[3,48,384]{2,1,0:T(8,128)}, u32[]{:S(2)}, u32[]{:S(2)}) collective-permute-start(f32[3,48,384]{2,1,0:T(8,128)S(1)} %bitcast.62), channel_id=1, source_target_pairs={{0,16},{16,0},{32,48},{48,32},{64,80},{80,64},{96,112},{112,96},{1... | collective-permute-start | bytes 663560 | tf_op jit(solution)/shard_map/ppermute | solution.py:25
  94.6 6.9 %shard_map.49.here_hbm = f32[768,384]{1,0:T(8,128)} custom-call(s32[12]{0:T(128)} %copy-done.6, s32[3,384]{1,0:T(4,128)} %pivots_ref.3, f32[768,384]{1,0:T(8,128)} %bitcast.48, f32[8,384,384]{2,1,0:T(8,128)} %bitcast.65), custom_call_target="tpu_custom_call" | custom-call | flops 2038431744 | bytes 5242880 | tf_op jit(solution)/shard_map/pallas_call | solution.py:380
  102.6 7.5 %collective-permute-done.26.refs_3_ = f32[3,2,48,384]{3,2,1,0:T(8,128)S(1)} collective-permute-done((f32[3,2,48,384]{3,2,1,0:T(8,128)S(1)}, f32[3,2,48,384]{3,2,1,0:T(8,128)S(1)}, u32[]{:S(2)}, u32[]{:S(2)}) %collective-permute-start.26) | collective-permute-done | bytes 442400 | tf_op jit(solution)/shard_map/ppermute | solution.py:21
  112.0 2.4 %collective-permute-done.34.refs_15_ = f32[3,48,384]{2,1,0:T(8,128)S(1)} collective-permute-done((f32[3,48,384]{2,1,0:T(8,128)}, f32[3,48,384]{2,1,0:T(8,128)S(1)}, u32[]{:S(2)}, u32[]{:S(2)}) %collective-permute-start.34) | collective-permute-done | bytes 221216 | tf_op jit(solution)/shard_map/ppermute | solution.py:25
  116.3 15.1 %shard_map.50 = (f32[1152,384]{1,0:T(8,128)}, f32[384,384]{1,0:T(8,128)}) custom-call(s32[12]{0:T(128)} %copy-done.6, f32[3,2,48,384]{3,2,1,0:T(8,128)} %copy-done.12, f32[3,2,48,384]{3,2,1,0:T(8,128)} %copy-done.16, f32[3,2,48,384]{3,2,1,0:T(8,128)} %copy-done.17, f32[3,2,48,384]{3,2,1,0:T(8,128)} %copy-done.18, f32[3,2,48,384]{3,2,1,0:T(8,128)} %copy-done.19, ...), custom_call_target="tpu_custom_call" | custom-call | flops 6794772480 | bytes 11534336 | tf_op jit(solution)/shard_map/pallas_call | solution.py:392
  131.4 8.2 %shard_map.51 = f32[768,384]{1,0:T(8,128)} custom-call(s32[12]{0:T(128)} %copy-done.6, f32[1152,768]{1,0:T(8,128)} %all-gather.5.cloned.1.call-done.panel_hbm, f32[1152,384]{1,0:T(8,128)} %get-tuple-element.96.basis_hbm, f32[768,384]{1,0:T(8,128)} %shard_map.49.here_hbm, f32[384,384]{1,0:T(8,128)} %get-tuple-element.98.head_hbm), custom_call_target="tpu_custom_call" | custom-call | flops 2038431744 | bytes 8388608 | tf_op jit(solution)/shard_map/pallas_call | solution.py:406
  (135 shorter events, 27.1 us)
Async XLA Ops:
  6.5 88.1 %all-gather.7.cloned.1.call-start = ((), (), s32[]{:S(2)}) async-start(), calls=%async_computation.1 | async-start | bytes 5308416 | tf_op jit(solution)/shard_map/all_gather | solution.py:307
  8.6 122.8 %all-gather.5.cloned.1.call-start = ((), (), s32[]{:S(2)}) async-start(), calls=%async_computation | async-start | bytes 3760128 | tf_op jit(solution)/shard_map/all_gather | solution.py:359
  9.0 13.2 %collective-permute-start = (f32[96,768]{0,1:T(8,128)S(1)}, f32[96,768]{0,1:T(8,128)S(1)}, u32[]{:S(2)}, u32[]{:S(2)}) collective-permute-start(f32[96,768]{0,1:T(8,128)S(1)} %get-tuple-element.101), channel_id=1, source_target_pairs={{0,4},{1,5},{2,6},{16,20},{17,21},{18,22},{32,36},{33,37},{34,38},... | collective-permute-start | bytes 884744 | tf_op jit(solution)/shard_map/ppermute | solution.py:35
  12.6 16.2 %collective-permute-start.1 = (f32[96,768]{0,1:T(8,128)S(1)}, f32[96,768]{0,1:T(8,128)S(1)}, u32[]{:S(2)}, u32[]{:S(2)}) collective-permute-start(f32[96,768]{0,1:T(8,128)S(1)} %get-tuple-element.100), channel_id=1, source_target_pairs={{0,8},{1,9},{2,10},{16,24},{17,25},{18,26},{32,40},{33,41},{34,42}... | collective-permute-start | bytes 884744 | tf_op jit(solution)/shard_map/ppermute | solution.py:35
  15.2 13.5 %collective-permute-start.2 = (f32[96,768]{0,1:T(8,128)S(1)}, f32[96,768]{0,1:T(8,128)S(1)}, u32[]{:S(2)}, u32[]{:S(2)}) collective-permute-start(f32[96,768]{0,1:T(8,128)S(1)} %get-tuple-element.99), channel_id=1, source_target_pairs={{0,12},{1,13},{2,14},{16,28},{17,29},{18,30},{32,44},{33,45},{34,4... | collective-permute-start | bytes 884744 | tf_op jit(solution)/shard_map/ppermute | solution.py:35
  28.8 9.5 %collective-permute-start.6 = (f32[576,384]{1,0:T(8,128)}, f32[576,384]{1,0:T(8,128)}, u32[]{:S(2)}, u32[]{:S(2)}) collective-permute-start(f32[576,384]{1,0:T(8,128)} %get-tuple-element.57), channel_id=1, source_target_pairs={{0,16},{16,0},{32,48},{48,32},{64,80},{80,64},{96,112},{112,96},{1... | collective-permute-start | bytes 2654216 | tf_op jit(solution)/shard_map/ppermute | solution.py:25
  38.4 8.4 %collective-permute-start.7 = (f32[72,384]{1,0:T(8,128)S(1)}, f32[72,384]{1,0:T(8,128)S(1)}, u32[]{:S(2)}, u32[]{:S(2)}) collective-permute-start(f32[72,384]{1,0:T(8,128)S(1)} %slice.57), channel_id=1, source_target_pairs={{0,32},{16,48},{32,64},{48,80},{64,96},{80,112},{96,0},{112,16},{1... | collective-permute-start | bytes 331784 | tf_op jit(solution)/shard_map/ppermute | solution.py:21
  39.7 7.1 %collective-permute-start.8 = (f32[72,384]{1,0:T(8,128)S(1)}, f32[72,384]{1,0:T(8,128)S(1)}, u32[]{:S(2)}, u32[]{:S(2)}) collective-permute-start(f32[72,384]{1,0:T(8,128)S(1)} %slice.57), channel_id=1, source_target_pairs={{0,64},{16,80},{32,96},{48,112},{64,0},{80,16},{96,32},{112,48},{1... | collective-permute-start | bytes 331784 | tf_op jit(solution)/shard_map/ppermute | solution.py:21
  44.1 7.0 %collective-permute-start.10 = (f32[144,384]{1,0:T(8,128)S(1)}, f32[144,384]{1,0:T(8,128)S(1)}, u32[]{:S(2)}, u32[]{:S(2)}) collective-permute-start(f32[144,384]{1,0:T(8,128)S(1)} %get-tuple-element.104), channel_id=1, source_target_pairs={{0,32},{16,48},{32,64},{48,80},{64,96},{80,112},{96,0},{112,16},{1... | collective-permute-start | bytes 663560 | tf_op jit(solution)/shard_map/ppermute | solution.py:21
  44.1 7.5 %collective-permute-start.11 = (f32[144,384]{1,0:T(8,128)S(1)}, f32[144,384]{1,0:T(8,128)S(1)}, u32[]{:S(2)}, u32[]{:S(2)}) collective-permute-start(f32[144,384]{1,0:T(8,128)S(1)} %get-tuple-element.103), channel_id=1, source_target_pairs={{0,64},{16,80},{32,96},{48,112},{64,0},{80,16},{96,32},{112,48},{1... | collective-permute-start | bytes 663560 | tf_op jit(solution)/shard_map/ppermute | solution.py:21
  46.8 10.1 %collective-permute-start.12 = (f32[144,384]{1,0:T(8,128)S(1)}, f32[144,384]{1,0:T(8,128)S(1)}, u32[]{:S(2)}, u32[]{:S(2)}) collective-permute-start(f32[144,384]{1,0:T(8,128)S(1)} %get-tuple-element.102), channel_id=1, source_target_pairs={{0,96},{16,112},{32,0},{48,16},{64,32},{80,48},{96,64},{112,80},{1... | collective-permute-start | bytes 663560 | tf_op jit(solution)/shard_map/ppermute | solution.py:21
  46.9 10.0 %collective-permute-start.13 = (f32[72,384]{1,0:T(8,128)S(1)}, f32[72,384]{1,0:T(8,128)S(1)}, u32[]{:S(2)}, u32[]{:S(2)}) collective-permute-start(f32[72,384]{1,0:T(8,128)S(1)} %get-tuple-element.106.a_ref), channel_id=1, source_target_pairs={{0,16},{16,0},{32,48},{48,32},{64,80},{80,64},{96,112},{112,96},{1... | collective-permute-start | bytes 331784 | tf_op jit(solution)/shard_map/ppermute | solution.py:25
  60.1 7.8 %collective-permute-start.15 = (f32[2,48,384]{2,1,0:T(8,128)S(1)}, f32[2,48,384]{2,1,0:T(8,128)S(1)}, u32[]{:S(2)}, u32[]{:S(2)}) collective-permute-start(f32[2,48,384]{2,1,0:T(8,128)S(1)} %fusion.5), channel_id=1, source_target_pairs={{0,4},{1,5},{2,6},{16,20},{17,21},{18,22},{32,36},{33,37},{34,38},... | collective-permute-start | bytes 442376 | tf_op jit(solution)/shard_map/ppermute | solution.py:35
  70.0 8.5 %collective-permute-start.18 = (f32[2,48,384]{2,1,0:T(8,128)S(1)}, f32[2,48,384]{2,1,0:T(8,128)S(1)}, u32[]{:S(2)}, u32[]{:S(2)}) collective-permute-start(f32[2,48,384]{2,1,0:T(8,128)S(1)} %add_add_fusion), channel_id=1, source_target_pairs={{0,1},{1,2},{2,3},{3,0},{4,5},{5,6},{6,7},{7,4},{8,9},{9,10},{10,1... | collective-permute-start | bytes 442376 | tf_op jit(solution)/shard_map/ppermute | solution.py:29
  71.8 15.6 %collective-permute-start.21 = (f32[3,48,384]{2,1,0:T(8,128)S(1)}, f32[3,48,384]{2,1,0:T(8,128)S(1)}, u32[]{:S(2)}, u32[]{:S(2)}) collective-permute-start(f32[3,48,384]{2,1,0:T(8,128)S(1)} %bitcast.59), channel_id=1, source_target_pairs={{0,32},{16,48},{32,64},{48,80},{64,96},{80,112},{96,0},{112,16},{1... | collective-permute-start | bytes 663560 | tf_op jit(solution)/shard_map/ppermute | solution.py:21
  71.8 15.6 %collective-permute-start.22 = (f32[3,48,384]{2,1,0:T(8,128)S(1)}, f32[3,48,384]{2,1,0:T(8,128)}, u32[]{:S(2)}, u32[]{:S(2)}) collective-permute-start(f32[3,48,384]{2,1,0:T(8,128)S(1)} %bitcast.60), channel_id=1, source_target_pairs={{0,64},{16,80},{32,96},{48,112},{64,0},{80,16},{96,32},{112,48},{1... | collective-permute-start | bytes 663560 | tf_op jit(solution)/shard_map/ppermute | solution.py:21
  73.9 13.6 %collective-permute-start.23 = (f32[3,48,384]{2,1,0:T(8,128)S(1)}, f32[3,48,384]{2,1,0:T(8,128)}, u32[]{:S(2)}, u32[]{:S(2)}) collective-permute-start(f32[3,48,384]{2,1,0:T(8,128)S(1)} %bitcast.61), channel_id=1, source_target_pairs={{0,96},{16,112},{32,0},{48,16},{64,32},{80,48},{96,64},{112,80},{1... | collective-permute-start | bytes 663560 | tf_op jit(solution)/shard_map/ppermute | solution.py:21
  78.5 8.9 %collective-permute-start.20 = (f32[2,48,384]{2,1,0:T(8,128)S(1)}, f32[2,48,384]{2,1,0:T(8,128)S(1)}, u32[]{:S(2)}, u32[]{:S(2)}) collective-permute-start(f32[2,48,384]{2,1,0:T(8,128)S(1)} %add_add_fusion), channel_id=1, source_target_pairs={{0,3},{1,0},{2,1},{3,2},{4,7},{5,4},{6,5},{7,6},{8,11},{9,8},{10,9... | collective-permute-start | bytes 442376 | tf_op jit(solution)/shard_map/ppermute | solution.py:29
  87.6 13.9 %collective-permute-start.24 = (f32[3,2,48,384]{3,2,1,0:T(8,128)S(1)}, f32[3,2,48,384]{3,2,1,0:T(8,128)S(1)}, u32[]{:S(2)}, u32[]{:S(2)}) collective-permute-start(f32[3,2,48,384]{3,2,1,0:T(8,128)S(1)} %slice.61.refs_0_), channel_id=1, source_target_pairs={{0,32},{16,48},{32,64},{48,80},{64,96},{80,112},{96,0},{112,16},{1... | collective-permute-start | bytes 1327112 | tf_op jit(solution)/shard_map/ppermute | solution.py:21
  87.7 14.9 %collective-permute-start.25 = (f32[3,2,48,384]{3,2,1,0:T(8,128)S(1)}, f32[3,2,48,384]{3,2,1,0:T(8,128)S(1)}, u32[]{:S(2)}, u32[]{:S(2)}) collective-permute-start(f32[3,2,48,384]{3,2,1,0:T(8,128)S(1)} %slice.61.refs_0_), channel_id=1, source_target_pairs={{0,64},{16,80},{32,96},{48,112},{64,0},{80,16},{96,32},{112,48},{1... | collective-permute-start | bytes 1327112 | tf_op jit(solution)/shard_map/ppermute | solution.py:21
  88.7 21.4 %collective-permute-start.26 = (f32[3,2,48,384]{3,2,1,0:T(8,128)S(1)}, f32[3,2,48,384]{3,2,1,0:T(8,128)S(1)}, u32[]{:S(2)}, u32[]{:S(2)}) collective-permute-start(f32[3,2,48,384]{3,2,1,0:T(8,128)S(1)} %slice.61.refs_0_), channel_id=1, source_target_pairs={{0,96},{16,112},{32,0},{48,16},{64,32},{80,48},{96,64},{112,80},{1... | collective-permute-start | bytes 1327112 | tf_op jit(solution)/shard_map/ppermute | solution.py:21
  89.2 21.9 %collective-permute-start.31 = (f32[3,48,384]{2,1,0:T(8,128)S(1)}, f32[3,48,384]{2,1,0:T(8,128)}, u32[]{:S(2)}, u32[]{:S(2)}) collective-permute-start(f32[3,48,384]{2,1,0:T(8,128)S(1)} %bitcast.62), channel_id=1, source_target_pairs={{0,16},{16,0},{32,48},{48,32},{64,80},{80,64},{96,112},{112,96},{1... | collective-permute-start | bytes 663560 | tf_op jit(solution)/shard_map/ppermute | solution.py:25
  94.6 16.9 %collective-permute-start.32 = (f32[3,48,384]{2,1,0:T(8,128)S(1)}, f32[3,48,384]{2,1,0:T(8,128)}, u32[]{:S(2)}, u32[]{:S(2)}) collective-permute-start(f32[3,48,384]{2,1,0:T(8,128)S(1)} %collective-permute-done.21.refs_9_), channel_id=1, source_target_pairs={{0,16},{16,0},{32,48},{48,32},{64,80},{80,64},{96,112},{112,96},{1... | collective-permute-start | bytes 663560 | tf_op jit(solution)/shard_map/ppermute | solution.py:25
  101.5 10.0 %collective-permute-start.33 = (f32[3,48,384]{2,1,0:T(8,128)}, f32[3,48,384]{2,1,0:T(8,128)S(1)}, u32[]{:S(2)}, u32[]{:S(2)}) collective-permute-start(f32[3,48,384]{2,1,0:T(8,128)} %collective-permute-done.22.refs_10_), channel_id=1, source_target_pairs={{0,16},{16,0},{32,48},{48,32},{64,80},{80,64},{96,112},{112,96},{1... | collective-permute-start | bytes 663560 | tf_op jit(solution)/shard_map/ppermute | solution.py:25
  (39 other events, 260.0 us)
Sparse Core Ops, SparseCore 0:
  9.0 35.9 all-gather.6
  60.1 55.8 all-gather.4
